TPU v7x, 32 devices: a whole 2x2x4 slice. The times are simulated.
32 devices in a mesh: row: 8 (over z, y), col: 4 (over x, core).
Axes of the slice: x: 2, y: 2, z: 4, core: 2. Of those that a mesh axis runs over, the one named last changes fastest.
Arguments:
- rhs: float32 [32, 65536], P(None, ('row', 'col')), may hold values from -5 to 7
- coords: float32 [3, 65536], P(None, ('row', 'col')), may hold values from 0 to 8, as said below
- nugget: float32 [65536], P(('row', 'col')), may hold values from 1.5 to 3
- near_ids: int32 [128, 3], P(('row', 'col')), may hold values from -1 to 127, as said below
- basis: float32 [7, 128, 65536], P(None, None, ('row', 'col')), may hold values from -6 to 6
Outputs:
- solution: float32 [32, 65536], P(None, ('row', 'col'))
- residual: float32 [32, 65536], P(None, ('row', 'col'))
Inputs may be any that keep to these rules, and one draw needn't show every extreme that they name: `near_ids`: row i lists leaf i and some of the leaves i - 1 to i + 1 inside the range, each at most once, in any order; the other slots hold -1; the first and last leaf of each device's block of 4 list all such leaves inside the range. `coords`: each leaf's points lie in a unit box with an integer corner; consecutive leaves lie in boxes that share a face.
All inputs are finite; a program needn't handle non-finite values.
Results may differ from a plain program's by a relative error of at most 0.0003.
Values sent between devices are 32-bit elements; how exact they have to be, the bound alone decides.
No kernel may reach another device: no remote copies, remote signals or barrier semaphores. Data moves between devices by JAX's collectives and lax.ppermute only.
A program may use at most 128 MiB of HBM per device.

v0:
```python
import functools

import jax
import jax.numpy as jnp
from jax import lax
from jax.experimental import pallas as pl
from jax.experimental.pallas import tpu as pltpu
from jax.sharding import PartitionSpec as P

LEAF = 512
ITERS = 4
WIN = 3
LANES = 128
LOCAL = 3
EDGE_BLOCKS = LEAF // LANES
CHUNK = 16
NORM_TILE = 8
PRODUCTS_TILE = 16
FLOPS = 3 * 10**9

root_three = 1.7320508075688772
spacing_factor = 1.6
matern_scale = root_three / (spacing_factor * LEAF ** (-1.0 / 3.0))

BOTH = ("row", "col")
ROWS_COLS = (((1,), (0,)), ((), ()))
ROWS_ROWS = (((1,), (1,)), ((), ()))

PAIRS = ("dq", "rq", "qq", "rw", "qw", "dw", "rz", "qz", "dz")


def halves(values):
    high = values.astype(jnp.bfloat16)
    low = (values - high.astype(jnp.float32)).astype(jnp.bfloat16)
    return high, low


def stacked(values):
    return jnp.concatenate(halves(values), axis=0)


def product(stack, high, low, dims):
    rows = stack.shape[0] // 2
    main = lax.dot_general(stack, high, dims, preferred_element_type=jnp.float32)
    rest = lax.dot_general(stack[:rows], low, dims, preferred_element_type=jnp.float32)
    return main[:rows] + (main[rows:] + rest)


def row_sum(values):
    return jnp.sum(values, axis=1, keepdims=True)


def in_lanes(columns, shape):
    lane = lax.broadcasted_iota(jnp.int32, shape, 1)
    block = jnp.zeros(shape, jnp.float32)
    for index, column in enumerate(columns):
        block = jnp.where(lane == index, column, block)
    return block


def sums_tile(columns, rows, depth):
    turned = in_lanes(columns, (rows, LANES)).T[:depth]
    return jnp.concatenate([turned, jnp.zeros((depth, LANES - rows), jnp.float32)], axis=1)


def level_terms(core, columns, rows, depth):
    twice = [jnp.concatenate([column, column], axis=0) for column in columns]
    zero = jnp.zeros((rows, 1), jnp.float32)
    tile = sums_tile([zero] * (len(PAIRS) - len(columns)) + twice, rows, depth)
    lane = lax.broadcasted_iota(jnp.int32, tile.shape, 1)
    return jnp.where(lane // (rows // 2) == core, tile, 0.0)


def chosen(core, odd, even):
    return jnp.where(core == 1, odd, even)


def whole(memory=pltpu.VMEM):
    return pl.BlockSpec(memory_space=memory)


def call(body, outs, *args, scalars=0, flops=0, limit=32):
    return pl.pallas_call(
        body,
        out_shape=outs,
        in_specs=[whole(pltpu.SMEM)] * scalars + [whole()] * (len(args) - scalars),
        out_specs=[whole()] * len(outs),
        compiler_params=pltpu.CompilerParams(vmem_limit_bytes=limit * 2**20),
        cost_estimate=pl.CostEstimate(flops=flops, bytes_accessed=2**20, transcendentals=0),
    )(*args)


def f32(*shape):
    return jax.ShapeDtypeStruct(shape, jnp.float32)


def bf16(*shape):
    return jax.ShapeDtypeStruct(shape, jnp.bfloat16)


def matrix_rows(rows, lanes):
    square = None
    for axis in range(3):
        spread = rows[:, axis : axis + 1] - lanes[axis : axis + 1]
        square = spread * spread if square is None else square + spread * spread
    square = square * (matern_scale * matern_scale)
    scaled = square * lax.rsqrt(jnp.maximum(square, 1e-30))
    return halves((1.0 + scaled) * jnp.exp(-scaled))


def fill_matrices(pairs, lane_ref, sub_ref, high_ref, low_ref):
    for matrix, (row_leaf, col_leaf) in enumerate(pairs):
        lanes = lane_ref[:, col_leaf * LEAF : (col_leaf + 1) * LEAF]

        def one(part, carry):
            row_at = pl.multiple_of(row_leaf * LEAF + part * CHUNK, CHUNK)
            out_at = pl.ds(pl.multiple_of(part * CHUNK, CHUNK), CHUNK)
            values = matrix_rows(sub_ref[pl.ds(row_at, CHUNK)], lanes)
            high_ref[matrix, out_at], low_ref[matrix, out_at] = values
            return carry

        lax.fori_loop(0, LEAF // CHUNK, one, 0, unroll=4)


def setup_kernel(pairs, lane_ref, basis_ref, high_ref, low_ref, basis_high_ref, basis_low_ref, sub_ref, raw_ref, sem_ref):
    levels, rank, _ = basis_ref.shape
    copies = [pltpu.make_async_copy(basis_ref.at[at], raw_ref.at[at], sem_ref.at[at]) for at in range(levels)]
    for copy in copies:
        copy.start()
    lanes = lane_ref[...]
    sub_ref[...] = jnp.concatenate([lanes, jnp.zeros((8 - lanes.shape[0], lanes.shape[1]), jnp.float32)], axis=0).T
    fill_matrices(pairs, lane_ref, sub_ref, high_ref, low_ref)
    for at, copy in enumerate(copies):
        copy.wait()
        here = slice(at * rank, (at + 1) * rank)
        basis_high_ref[here], basis_low_ref[here] = halves(raw_ref[at])


def edge_matrices(core_ref, rows, sub_ref, paired_ref, other_ref, high_ref, low_ref):
    core = core_ref[0]
    leaves = sub_ref.shape[0] // LEAF
    paired = paired_ref[:3]
    other = other_ref[rows : rows + 3]
    lanes = [chosen(core, paired, other), chosen(core, other, paired)]

    for side in range(2):
        first_row = side * (leaves - 1) * LEAF

        def one(part, carry):
            row_at = pl.multiple_of(first_row + part * CHUNK, CHUNK)
            out_at = pl.ds(pl.multiple_of(part * CHUNK, CHUNK), CHUNK)
            values = matrix_rows(sub_ref[pl.ds(row_at, CHUNK)], lanes[side])
            high_ref[side, out_at], low_ref[side, out_at] = values
            return carry

        lax.fori_loop(0, LEAF // CHUNK, one, 0, unroll=4)


def sides(core, field_ref):
    head = field_ref[:, :LEAF]
    tail = field_ref[:, field_ref.shape[1] - LEAF :]
    return chosen(core, head, tail), chosen(core, tail, head)


def edges_kernel(core_ref, field_ref, coords_ref, paired_ref, other_ref):
    core = core_ref[0]
    pad = jnp.zeros((8 - 3, LEAF), jnp.float32)
    paired, other = sides(core, coords_ref)
    paired_ref[...] = jnp.concatenate([paired, pad], axis=0)
    other_ref[...] = jnp.concatenate([sides(core, field_ref)[1], other, pad], axis=0)


def down_kernel(core_ref, field_ref, high_ref, low_ref, local_ref, keep_ref, send_ref, *tile_refs):
    core = core_ref[0]
    rank = LANES
    rows, width = field_ref.shape
    half = width // 2
    stack = stacked(field_ref[...])
    for part in range(2):
        points = slice(part * half, (part + 1) * half)
        local_ref[:, part * rank : (part + 1) * rank] = product(
            stack[:, points], high_ref[:rank, points], low_ref[:rank, points], ROWS_ROWS
        )
    all_points = product(stack, high_ref[rank:], low_ref[rank:], ROWS_ROWS)
    local_ref[:, 2 * rank :] = all_points[:, :rank]
    own = rows // 2
    for bit in range(all_points.shape[1] // rank - 1):
        block = all_points[:, (bit + 1) * rank : (bit + 2) * rank]
        keep_ref[bit * own : (bit + 1) * own] = chosen(core, block[own:], block[:own])
        at = EDGE_BLOCKS * rows + bit * own
        send_ref[at : at + own] = chosen(core, block[:own], block[own:])
    paired = sides(core, field_ref)[0]
    for block in range(EDGE_BLOCKS):
        send_ref[block * rows : (block + 1) * rows] = paired[:, block * LANES : (block + 1) * LANES]
    for ref in tile_refs:
        ref[...] = sums_tile([row_sum(field_ref[...] * field_ref[...])], rows, NORM_TILE)


def leaf_of(ref, leaf):
    return ref[:, leaf * LEAF : (leaf + 1) * LEAF]


def weight_of(weights_ref, leaf, offset):
    at = WIN * leaf + offset + 1
    return weights_ref[at : at + 1]


def leaf_weights(near_ids, first_leaf):
    target = first_leaf + jnp.arange(near_ids.shape[0])[:, None] + jnp.arange(WIN)[None, :] - 1
    found = jnp.any(near_ids[:, None, :] == target[:, :, None], axis=2) & (target >= 0)
    weights = jnp.where(found, 1.0 / (16 * WIN), 0.0).astype(jnp.float32)
    return jnp.broadcast_to(weights.reshape(-1, 1), (weights.size, LEAF))


def inner_kernel(half, weights_ref, field_ref, nugget_ref, high_ref, low_ref, pair_high_ref, pair_low_ref, out_ref):
    leaves = weights_ref.shape[0] // WIN
    start = half * (leaves // 2)
    stop = start + leaves // 2
    pieces = {leaf: stacked(leaf_of(field_ref, leaf)) for leaf in range(max(start - 1, 0), min(stop + 1, leaves))}
    for leaf in range(start, stop):
        at = leaf - start
        inside = product(pieces[leaf], high_ref[at], low_ref[at], ROWS_COLS)
        total = leaf_of(nugget_ref, leaf) * leaf_of(field_ref, leaf) + weight_of(weights_ref, leaf, 0) * inside
        if leaf > 0:
            before = product(pieces[leaf - 1], pair_high_ref[leaf - 1], pair_low_ref[leaf - 1], ROWS_COLS)
            total = total + weight_of(weights_ref, leaf, -1) * before
        if leaf < leaves - 1:
            after = product(pieces[leaf + 1], pair_high_ref[leaf], pair_low_ref[leaf], ROWS_ROWS)
            total = total + weight_of(weights_ref, leaf, 1) * after
        out_ref[:, at * LEAF : (at + 1) * LEAF] = total


def edge_kernel(sums, *refs):
    core_ref, weights_ref, paired_ref, other_ref, high_ref, low_ref, front_ref, back_ref = refs[:8]
    refs = refs[8:]
    out_ref = refs[-2] if sums else refs[-1]
    core = core_ref[0]
    rows, width = out_ref.shape
    leaves = width // LEAF
    paired = [paired_ref[block * rows : (block + 1) * rows] for block in range(EDGE_BLOCKS)]
    paired = jnp.concatenate(paired, axis=1)
    before = chosen(core, paired, other_ref[:rows])
    after = chosen(core, other_ref[:rows], paired)
    out_ref[:, : width // 2] = front_ref[...]
    out_ref[:, width // 2 :] = back_ref[...]
    part = product(stacked(before), high_ref[0], low_ref[0], ROWS_ROWS)
    out_ref[:, :LEAF] += weight_of(weights_ref, 0, -1) * part
    part = product(stacked(after), high_ref[1], low_ref[1], ROWS_ROWS)
    out_ref[:, width - LEAF :] += weight_of(weights_ref, leaves - 1, 1) * part
    if not sums:
        return
    fields = dict(zip("rqdw", refs[:4]))
    locals_ = dict(zip("rqd", refs[4:7]))
    tile_ref = refs[-1]
    totals = {pair: jnp.zeros((rows, 1), jnp.float32) for pair in PAIRS}
    for leaf in range(leaves):
        here = {name: leaf_of(ref, leaf) for name, ref in fields.items()}
        here["z"] = leaf_of(out_ref, leaf)
        for left, right in PAIRS:
            totals[left + right] = totals[left + right] + row_sum(here[left] * here[right])
    for block in range(LOCAL):
        scale = 1.0 / (LEAF * (2 if block < 2 else 4))
        lanes = slice(block * LANES, (block + 1) * LANES)
        for name in "rqd":
            term = row_sum(locals_[name][:, lanes] * locals_["q"][:, lanes])
            totals[name + "z"] = totals[name + "z"] + scale * term
    tile_ref[...] = sums_tile([totals[pair] for pair in PAIRS], rows, PRODUCTS_TILE)


def first_combine_kernel(products, cluster, *refs):
    core_ref, mine_ref, other_ref, tile_ref = refs[:4]
    message_ref, level_ref = refs[-2:]
    own = level_ref.shape[0]
    depth = tile_ref.shape[0]
    total = mine_ref[...] + other_ref[EDGE_BLOCKS * 2 * own :]
    level = total[:own]
    level_ref[...] = level
    tile = tile_ref[...]
    if products:
        partners = [refs[4][:own], level, refs[5][:own]]
        columns = [row_sum(level * partner) * (1.0 / cluster) for partner in partners]
        tile = tile + level_terms(core_ref[0], columns, 2 * own, depth)
    left = total.shape[0] - own
    message_ref[:left] = total[own:]
    message_ref[left:] = tile


def combine_kernel(products, last, sibling, own, bits, clusters, *refs):
    refs = list(refs)
    core_ref, mine_ref = refs[:2]
    got = [ref[...] for ref in refs[2 : 2 + 2 ** len(bits) - 1]]
    refs = refs[1 + 2 ** len(bits) :]
    sibling_ref = refs.pop() if sibling else None
    level_out = [] if last else [refs.pop() for _ in bits][::-1]
    next_ref = refs.pop()
    depth = PRODUCTS_TILE if products else NORM_TILE
    near = mine_ref[...] + got[0]
    total = near
    pairs = [(near[:own], bits[0], 0, clusters[0])]
    if len(bits) == 2:
        far = got[1] + got[2]
        total = near + far
        if sibling:
            sibling_ref[...] = far[:own]
        pairs.append((far[:own], None, 1, clusters[0]))
        pairs.append((total[own : 2 * own], bits[1], 0, clusters[1]))
    for ref, pair in zip(level_out, pairs[:: 2 if len(bits) == 2 else 1]):
        ref[...] = pair[0]
    tile = total[total.shape[0] - depth :]
    if products:
        r_ref, d_ref = refs[:2]
        refs = refs[2:]
        siblings = [refs.pop(0), refs.pop(0)] if len(bits) == 2 else []
        columns = [jnp.zeros((own, 1), jnp.float32)] * 3
        for level, bit, kind, cluster in pairs:
            if kind:
                partners = [siblings[0][...], level, siblings[1][...]]
            else:
                here = slice(bit * own, (bit + 1) * own)
                partners = [r_ref[here], level, d_ref[here]]
            terms = [row_sum(level * partner) * (1.0 / cluster) for partner in partners]
            columns = [column + term for column, term in zip(columns, terms)]
        tile = tile + level_terms(core_ref[0], columns, 2 * own, depth)
    left = total.shape[0] - depth - len(bits) * own
    if not last:
        next_ref[:left] = total[len(bits) * own : len(bits) * own + left]
        next_ref[left:] = tile
    else:
        for index, ref in enumerate(refs):
            next_ref[index * own : (index + 1) * own] = ref[...]
        for bit, pair in zip(bits, pairs[:: 2 if len(bits) == 2 else 1]):
            next_ref[bit * own : (bit + 1) * own] = pair[0]
        next_ref[next_ref.shape[0] - depth :] = tile


def up_parts(core, mine_ref, other_ref, local_ref, rows, width, depth):
    own = rows // 2
    crossing = (mine_ref.shape[0] - depth) // own
    sums = (mine_ref[crossing * own :] + other_ref[crossing * own :]).T[:rows]
    scaled = []
    for bit in range(crossing):
        here = slice(bit * own, (bit + 1) * own)
        low_rows = chosen(core, other_ref[here], mine_ref[here])
        high_rows = chosen(core, mine_ref[here], other_ref[here])
        scaled.append(jnp.concatenate([low_rows, high_rows], axis=0) * (1.0 / (width * (2 << bit))))
    one = [local_ref[:, part * LANES : (part + 1) * LANES] * (1.0 / (2 * LEAF)) for part in range(2)]
    two = local_ref[:, 2 * LANES :] * (1.0 / (4 * LEAF))
    return sums, [stacked(jnp.concatenate([one[part], two] + scaled, axis=1)) for part in range(2)]


def own_rows(core, column, crossing):
    own = column.shape[0] // 2
    return jnp.concatenate([chosen(core, column[own:], column[:own])] * crossing, axis=0)


def residual_up_kernel(first, siblings, *refs):
    core_ref, high_ref, low_ref, near_ref, mine_ref, other_ref, local_ref = refs[:7]
    refs = refs[7:]
    if first:
        image_ref, state_ref, send_ref = refs
        q_ref = image_ref
    else:
        field_ref, old_d_ref, old_q_ref, old_skel_ref, old_local_ref, old_state_ref = refs[:6]
        r_siblings = refs[6 : 6 + siblings]
        d_siblings = refs[6 + siblings : 6 + 2 * siblings]
        refs = refs[6 + 2 * siblings :]
        image_ref, state_ref, send_ref, d_ref, q_ref, skel_ref, new_local_ref = refs[:7]
        new_siblings = refs[7:]
    core = core_ref[0]
    rows, width = near_ref.shape
    half = width // 2
    sums, stacks = up_parts(core, mine_ref, other_ref, local_ref, rows, width, NORM_TILE)
    norm = sums[:, 0:1]
    state_ref[...] = in_lanes([norm], (rows, LANES))
    ratio = None if first else norm / old_state_ref[:, 0:1]
    for part in range(2):
        points = slice(part * half, (part + 1) * half)
        image = near_ref[:, points] + product(stacks[part], high_ref[:, points], low_ref[:, points], ROWS_COLS)
        image_ref[:, points] = image
        if not first:
            d_ref[:, points] = field_ref[:, points] + ratio * old_d_ref[:, points]
            q_ref[:, points] = image + ratio * old_q_ref[:, points]
    send_ref[...] = sides(core, q_ref)[1]
    if not first:
        rows_in = skel_ref.shape[0]
        crossing = rows_in // (rows // 2)
        skel_ref[...] = mine_ref[:rows_in] + own_rows(core, ratio, crossing) * old_skel_ref[...]
        new_local_ref[...] = local_ref[...] + ratio * old_local_ref[...]
        own_ratio = own_rows(core, ratio, 1)
        for new_ref, r_ref, d_ref in zip(new_siblings, r_siblings, d_siblings):
            new_ref[...] = r_ref[...] + own_ratio * d_ref[...]


def image_up_kernel(first, last, siblings, *refs):
    core_ref, high_ref, low_ref, near_ref, mine_ref, other_ref, local_ref = refs[:7]
    r_ref, w_ref, d_ref, q_ref, state_ref = refs[7:12]
    refs = refs[12:]
    if not first:
        solution_ref = refs[0]
        refs = refs[1:]
    if not last:
        r_skel_ref, d_skel_ref, r_local_ref, d_local_ref = refs[:4]
        r_siblings, q_siblings, d_siblings = [
            refs[4 + index * siblings : 4 + (index + 1) * siblings] for index in range(3)
        ]
        refs = refs[4 + 3 * siblings :]
    new_solution_ref, new_r_ref = refs[:2]
    if not last:
        new_d_ref, new_q_ref, new_skel_ref, new_local_ref, new_state_ref, send_ref = refs[2:8]
        new_siblings = refs[8:]
    core = core_ref[0]
    rows, width = near_ref.shape
    half = width // 2
    sums, stacks = up_parts(core, mine_ref, other_ref, local_ref, rows, width, PRODUCTS_TILE)
    dot = {pair: sums[:, index : index + 1] for index, pair in enumerate(PAIRS)}
    norm = state_ref[:, 0:1]
    step = norm / dot["dq"]
    new_norm = norm - step * (2.0 * dot["rq"] - step * dot["qq"])
    ratio = new_norm / norm
    curve = dot["rw"] - step * (dot["qw"] + dot["rz"] - step * dot["qz"])
    curve = curve + ratio * (dot["dw"] - step * dot["dz"] + dot["rq"] - step * dot["qq"] + ratio * dot["dq"])
    new_step = new_norm / curve
    for part in range(2):
        points = slice(part * half, (part + 1) * half)
        image = near_ref[:, points] + product(stacks[part], high_ref[:, points], low_ref[:, points], ROWS_COLS)
        d = d_ref[:, points]
        q = q_ref[:, points]
        r = r_ref[:, points] - step * q
        new_q = w_ref[:, points] - step * image + ratio * q
        new_d = r + ratio * d
        moved = step * d + new_step * new_d
        new_solution_ref[:, points] = moved if first else solution_ref[:, points] + moved
        new_r_ref[:, points] = r - new_step * new_q
        if not last:
            new_d_ref[:, points] = new_d
            new_q_ref[:, points] = new_q
    if not last:
        rows_in = new_skel_ref.shape[0]
        crossing = rows_in // (rows // 2)
        r_skel = r_skel_ref[:rows_in] - own_rows(core, step, crossing) * mine_ref[:rows_in]
        new_skel_ref[...] = r_skel + own_rows(core, ratio, crossing) * d_skel_ref[:rows_in]
        new_local_ref[...] = r_local_ref[...] - step * local_ref[...] + ratio * d_local_ref[...]
        own_step, own_ratio = own_rows(core, step, 1), own_rows(core, ratio, 1)
        for new_ref, r_ref, q_ref, d_ref in zip(new_siblings, r_siblings, q_siblings, d_siblings):
            new_ref[...] = r_ref[...] - own_step * q_ref[...] + own_ratio * d_ref[...]
        new_state_ref[...] = in_lanes([new_norm], (rows, LANES))
        send_ref[...] = sides(core, new_r_ref)[1]


def per_device(rhs, coords, nugget, near_ids, basis):
    rows, width = rhs.shape
    levels = basis.shape[0]
    leaves = width // LEAF
    own = rows // 2
    crossing = levels - (leaves.bit_length() - 1)
    devices = lax.axis_size("row") * lax.axis_size("col")
    place = jnp.reshape(lax.axis_index(BOTH), (1,))
    core = place % 2
    nugget = nugget[None, :]
    weights = leaf_weights(near_ids, place[0] * leaves)

    stages = [list(range(bit, min(bit + 2, crossing))) for bit in range(1, crossing, 2)]
    siblings = sum(len(bits) == 2 for bits in stages)

    def swap(value, mask):
        return lax.ppermute(value, BOTH, [(source, source ^ mask) for source in range(devices)])

    def halo(other):
        outward = [(index, index + 1) for index in range(1, devices - 1, 2)]
        ends = [(0, 0), (devices - 1, devices - 1)]
        return lax.ppermute(other, BOTH, outward + [(target, source) for source, target in outward] + ends)

    def down(field, *tile):
        shapes = [f32(rows, LOCAL * LANES), f32(crossing * own, LANES)]
        shapes = shapes + [f32(EDGE_BLOCKS * rows + crossing * own, LANES)] + list(tile)
        return call(down_kernel, shapes, core, field, high, low, scalars=1, flops=FLOPS)

    def inner(half, field):
        args = [weights, field, nugget, *diagonal[half], *beside]
        body = functools.partial(inner_kernel, half)
        return call(body, [f32(rows, width // 2)], *args, flops=FLOPS // 2)[0]

    def edge(paired, other, front, back, *more):
        shapes = [f32(rows, width)] + ([f32(PRODUCTS_TILE, LANES)] if more else [])
        args = [core, weights, paired, other, *outside, front, back, *more]
        return call(functools.partial(edge_kernel, bool(more)), shapes, *args, scalars=1, flops=FLOPS // 3)

    def chain(products, final, keep, got, tile, beside_steps, r_skel=None, d_skel=None, r_sib=(), d_sib=()):
        depth = PRODUCTS_TILE if products else NORM_TILE
        results = []
        both = [r_skel, d_skel] if products else []
        message, level = call(
            functools.partial(first_combine_kernel, products, 2 * width),
            [f32((crossing - 1) * own + depth, LANES), f32(own, LANES)],
            core,
            keep,
            got,
            tile,
            *both,
            scalars=1,
        )
        done, kept = [level], []
        for index in range(len(stages) + 1):
            bits = stages[index] if index < len(stages) else []
            masks = [sum(1 << bit for at, bit in enumerate(bits) if pick >> at & 1) for pick in range(1, 2 ** len(bits))]
            got = [swap(message, mask) for mask in masks or [1]]
            if index < len(beside_steps):
                *got, result = lax.optimization_barrier((*got, beside_steps[index](message)))
                results.append(result)
            if not bits:
                break
            left = crossing - bits[-1] - 1
            paired = len(bits) == 2
            args = [core, message, *got, *both]
            if products and paired:
                args = args + [r_sib[index], d_sib[index]]
            sibling = paired and not final
            clusters = [width * (2 << bit) for bit in bits]
            message, *levels_out = call(
                functools.partial(combine_kernel, products, not left, sibling, own, bits, clusters),
                [f32((left or crossing) * own + depth, LANES)] + [f32(own, LANES)] * ((len(bits) if left else 0) + sibling),
                *args,
                *([] if left else done),
                scalars=1,
            )
            kept = kept + levels_out[len(levels_out) - sibling :]
            done = done + levels_out[: len(levels_out) - sibling]
        return message, got[0], results, kept

    paired_coords, other = call(
        edges_kernel, [f32(8, LEAF), f32(rows + 8, LEAF)], core, rhs, coords, scalars=1
    )
    other = halo(other)
    paired_coords = swap(paired_coords, 1)
    half = leaves // 2
    pairs = [(leaf, leaf) for leaf in range(half)]
    *front_diagonal, high, low, turned = pl.pallas_call(
        functools.partial(setup_kernel, pairs),
        out_shape=[bf16(half, LEAF, LEAF)] * 2
        + [pltpu.VMEM((levels * LANES, width), jnp.bfloat16)] * 2
        + [f32(width, 8)],
        in_specs=[whole(), whole(pltpu.HBM)],
        out_specs=[whole()] * 5,
        scratch_shapes=[pltpu.VMEM(basis.shape, jnp.float32), pltpu.SemaphoreType.DMA((levels,))],
        compiler_params=pltpu.CompilerParams(vmem_limit_bytes=44 * 2**20),
        cost_estimate=pl.CostEstimate(flops=FLOPS, bytes_accessed=2**20, transcendentals=0),
    )(coords, basis)
    diagonal = [front_diagonal, None]
    beside = outside = None

    def after(message, *values):
        return lax.optimization_barrier((message, *values))[1:]

    def late_matrices(message):
        groups = [[(leaf, leaf) for leaf in range(half, leaves)], [(leaf, leaf + 1) for leaf in range(leaves - 1)]]

        def body(lane_ref, sub_ref, *refs):
            for index, group in enumerate(groups):
                fill_matrices(group, lane_ref, sub_ref, *refs[2 * index : 2 * index + 2])

        shapes = [bf16(len(group), LEAF, LEAF) for group in groups for _ in range(2)]
        return call(body, shapes, *after(message, coords, turned), flops=2 * FLOPS)

    def late_edge_matrices(message):
        def body(core_ref, *refs):
            edge_matrices(core_ref, rows, *refs)

        args = after(message, turned, paired_coords, other)
        return call(body, [bf16(2, LEAF, LEAF)] * 2, core, *args, scalars=1, flops=FLOPS)

    solution, r, carried = None, rhs, None
    for step in range(0, ITERS, 2):
        first, last = step == 0, step + 2 == ITERS
        r_local, keep, part, tile = down(r, f32(NORM_TILE, LANES))
        from_core = got = swap(part, 1)
        if first:
            message, got, results, r_sib = chain(False, False, keep, got, tile, [late_matrices, late_edge_matrices])
            diagonal[1], beside = results[0][:2], results[0][2:]
            outside = results[1]
            (near,) = edge(from_core, other, inner(0, r), inner(1, r))
        else:
            fronts = []

            def inner_work(message):
                fronts.extend(inner(half, *after(message, r)) for half in range(2))
                return fronts

            def edge_work(message):
                return edge(from_core, other, *after(message, *fronts))[0]

            message, got, results, r_sib = chain(False, False, keep, got, tile, [inner_work, edge_work])
            near = results[1]
        args = [core, high, low, near, message, got, r_local]
        outs = [f32(rows, width), f32(rows, LANES), f32(rows, LEAF)]
        if first:
            w, state, other = call(
                functools.partial(residual_up_kernel, True, 0), outs, *args, scalars=1, flops=FLOPS // 2
            )
            d, q, d_skel, d_local, d_sib = r, w, message, r_local, r_sib
        else:
            outs = outs + [f32(rows, width)] * 2 + [f32(crossing * own, LANES), f32(rows, LOCAL * LANES)]
            outs = outs + [f32(own, LANES)] * siblings
            body = functools.partial(residual_up_kernel, False, siblings)
            args = args + [r, *carried, *r_sib, *d_sib]
            w, state, other, d, q, d_skel, d_local, *d_sib = call(
                body, outs, *args, scalars=1, flops=FLOPS // 2
            )
        r_skel = message
        other = halo(other)
        q_local, keep, part = down(q)
        got = swap(part, 1)
        near, tile = edge(got, other, inner(0, q), inner(1, q), r, q, d, w, r_local, q_local, d_local)
        message, got, _, q_sib = chain(True, last, keep, got, tile, [], r_skel, d_skel, r_sib, d_sib)
        args = [core, high, low, near, message, got, q_local, r, w, d, q, state]
        args = args + ([] if first else [solution]) + ([] if last else [r_skel, d_skel, r_local, d_local, *r_sib, *q_sib, *d_sib])
        outs = [f32(rows, width)] * 2
        if not last:
            outs = outs + [f32(rows, width)] * 2 + [f32(crossing * own, LANES), f32(rows, LOCAL * LANES)]
            outs = outs + [f32(rows, LANES), f32(rows, LEAF)] + [f32(own, LANES)] * siblings
        solution, r, *rest = call(
            functools.partial(image_up_kernel, first, last, siblings), outs, *args, scalars=1, flops=FLOPS // 2
        )
        if not last:
            carried = rest[:5]
            other = halo(rest[5])
            d_sib = rest[6:]
    return (solution, r)


def solution(mesh):
    placed = (
        P(None, BOTH),
        P(None, BOTH),
        P(BOTH),
        P(BOTH, None),
        P(None, None, BOTH),
    )
    return jax.shard_map(
        per_device,
        mesh=mesh,
        in_specs=placed,
        out_specs=(P(None, BOTH), P(None, BOTH)),
        check_vma=False,
    )
```

profile of v0, /device:TPU:0, one launch (start us, length us, event | category | flops | bytes accessed | tf_op | source)
XLA Modules:
  0.0 122.2 jit_solution(12552628801436015041)
XLA Ops:
  4.4 5.0 %shard_map.68 = (bf16[2,512,512]{2,1,0:T(8,128)(2,1)S(1)}, bf16[2,512,512]{2,1,0:T(8,128)(2,1)S(1)}, bf16[896,2048]{1,0:T(8,128)(2,1)S(1)}, bf16[896,2048]{1,0:T(8,128)(2,1)S(1)}, f32[2048,8]{1,0:T(8,128)}) custom-call(f32[3,2048]{1,0:T(4,128)S(1)} %copy-done.8, f32[7,128,2048]{2,1,0:T(8,128)} %basis_ref.1), custom_call_target="tpu_custom_call" | custom-call | flops 3000000000 | bytes 1048576 | tf_op jit(solution)/shard_map/pallas_call | solution.py:537
  9.5 2.3 %shard_map.69 = (f32[32,384]{1,0:T(8,128)S(1)}, f32[80,128]{1,0:T(8,128)S(1)}, f32[208,128]{1,0:T(8,128)S(1)}, f32[8,128]{1,0:T(8,128)S(1)}) custom-call(s32[1]{0:T(128)S(6)} %select_n.15.core_ref.refs_0_, f32[32,2048]{1,0:T(8,128)S(1)} %copy-done.5, bf16[896,2048]{1,0:T(8,128)(2,1)S(1)} %get-tuple-element.111.high_ref.refs_1_, ...), custom_call_target="tpu_custom_call" | custom-call | flops 3000000000 | bytes 1048576 | tf_op jit(solution)/shard_map/pallas_call | solution.py:83
  12.4 3.9 %collective-permute-start = (f32[208,128]{1,0:T(8,128)S(1)}, f32[208,128]{1,0:T(8,128)S(1)}, u32[]{:S(2)}, u32[]{:S(2)}) collective-permute-start(f32[208,128]{1,0:T(8,128)S(1)} %get-tuple-element.113), channel_id=1, source_target_pairs={{0,1},{1,0},{2,3},{3,2},{4,5},{5,4},{6,7},{7,6},{8,9},{9,8},{10,11... | collective-permute-start | bytes 319496 | tf_op jit(solution)/shard_map/ppermute | solution.py:466
  17.2 2.5 %collective-permute-start.4 = (f32[72,128]{1,0:T(8,128)S(1)}, f32[72,128]{1,0:T(8,128)S(1)}, u32[]{:S(2)}, u32[]{:S(2)}) collective-permute-start(f32[72,128]{1,0:T(8,128)S(1)} %get-tuple-element.117.refs_1_), channel_id=1, source_target_pairs={{0,6},{1,7},{2,4},{3,5},{4,2},{5,3},{6,0},{7,1},{8,14},{9,15},{10,... | collective-permute-start | bytes 110600 | tf_op jit(solution)/shard_map/ppermute | solution.py:466
  22.0 6.7 %shard_map.72 = (bf16[2,512,512]{2,1,0:T(8,128)(2,1)S(1)}, bf16[2,512,512]{2,1,0:T(8,128)(2,1)S(1)}, bf16[3,512,512]{2,1,0:T(8,128)(2,1)S(1)}, bf16[3,512,512]{2,1,0:T(8,128)(2,1)S(1)}) custom-call(f32[3,2048]{1,0:T(4,128)S(1)} %copy-done.9, f32[2048,8]{1,0:T(8,128)S(1)} %copy-done.10), custom_call_target="tpu_custom_call" | custom-call | flops 6000000000 | bytes 1048576 | tf_op jit(solution)/shard_map/pallas_call | solution.py:83
  28.7 4.8 %collective-permute-start.7 = (f32[40,128]{1,0:T(8,128)S(1)}, f32[40,128]{1,0:T(8,128)S(1)}, u32[]{:S(2)}, u32[]{:S(2)}) collective-permute-start(f32[40,128]{1,0:T(8,128)S(1)} %get-tuple-element.128.refs_1_), channel_id=1, source_target_pairs={{0,24},{1,25},{2,26},{3,27},{4,28},{5,29},{6,30},{7,31},{8,16},{9,... | collective-permute-start | bytes 61448 | tf_op jit(solution)/shard_map/ppermute | solution.py:466
  34.2 2.7 %shard_map.74 = (bf16[2,512,512]{2,1,0:T(8,128)(2,1)S(1)}, bf16[2,512,512]{2,1,0:T(8,128)(2,1)S(1)}) custom-call(s32[1]{0:T(128)S(6)} %select_n.15.core_ref.refs_0_, f32[2048,8]{1,0:T(8,128)S(1)} %copy-done.11, f32[8,512]{1,0:T(8,128)S(1)} %collective-permute-done.8.refs_1_, f32[40,512]{1,0:T(8,128)S(1)} %collective-permute-done.1.refs_2_.refs_3_), custom_call_target="tpu_custom_call" | custom-call | flops 3000000000 | bytes 1048576 | tf_op jit(solution)/shard_map/pallas_call | solution.py:83
  43.8 2.3 %shard_map.80 = (f32[32,384]{1,0:T(8,128)S(1)}, f32[80,128]{1,0:T(8,128)S(1)}, f32[208,128]{1,0:T(8,128)S(1)}) custom-call(s32[1]{0:T(128)S(6)} %select_n.15.core_ref.refs_0_, f32[32,2048]{1,0:T(8,128)S(1)} %get-tuple-element.151.field_ref.refs_9_.refs_11_.refs_8_.refs_10_, bf16[896,2048]{1,0:T(8,128)(2,1)S(1)} %copy-done.1, bf16[896,2048]{1,0:T(8,128)(2,1)S(1)} %copy-done.3), custom_call_target="tpu_custom_call" | custom-call | flops 3000000000 | bytes 1048576 | tf_op jit(solution)/shard_map/pallas_call | solution.py:83
  47.0 1.9 %collective-permute-start.10 = (f32[208,128]{1,0:T(8,128)S(1)}, f32[208,128]{1,0:T(8,128)S(1)}, u32[]{:S(2)}, u32[]{:S(2)}) collective-permute-start(f32[208,128]{1,0:T(8,128)S(1)} %get-tuple-element.152), channel_id=1, source_target_pairs={{0,1},{1,0},{2,3},{3,2},{4,5},{5,4},{6,7},{7,6},{8,9},{9,8},{10,11... | collective-permute-start | bytes 319496 | tf_op jit(solution)/shard_map/ppermute | solution.py:466
  51.3 3.5 %collective-permute-start.14 = (f32[80,128]{1,0:T(8,128)S(1)}, f32[80,128]{1,0:T(8,128)S(1)}, u32[]{:S(2)}, u32[]{:S(2)}) collective-permute-start(f32[80,128]{1,0:T(8,128)S(1)} %get-tuple-element.158.refs_1_), channel_id=1, source_target_pairs={{0,6},{1,7},{2,4},{3,5},{4,2},{5,3},{6,0},{7,1},{8,14},{9,15},{10,... | collective-permute-start | bytes 122888 | tf_op jit(solution)/shard_map/ppermute | solution.py:466
  56.9 2.0 %collective-permute-done.13.refs_3_ = f32[80,128]{1,0:T(8,128)S(1)} collective-permute-done((f32[80,128]{1,0:T(8,128)S(1)}, f32[80,128]{1,0:T(8,128)S(1)}, u32[]{:S(2)}, u32[]{:S(2)}) %collective-permute-start.13) | collective-permute-done | bytes 40992 | tf_op jit(solution)/shard_map/ppermute | solution.py:466
  59.4 4.7 %collective-permute-start.17 = (f32[48,128]{1,0:T(8,128)S(1)}, f32[48,128]{1,0:T(8,128)S(1)}, u32[]{:S(2)}, u32[]{:S(2)}) collective-permute-start(f32[48,128]{1,0:T(8,128)S(1)} %get-tuple-element.160.refs_1_), channel_id=1, source_target_pairs={{0,24},{1,25},{2,26},{3,27},{4,28},{5,29},{6,30},{7,31},{8,16},{9,... | collective-permute-start | bytes 73736 | tf_op jit(solution)/shard_map/ppermute | solution.py:466
  66.0 2.9 %collective-permute-done.16.refs_3_ = f32[48,128]{1,0:T(8,128)S(1)} collective-permute-done((f32[48,128]{1,0:T(8,128)S(1)}, f32[48,128]{1,0:T(8,128)S(1)}, u32[]{:S(2)}, u32[]{:S(2)}) %collective-permute-start.16) | collective-permute-done | bytes 24608 | tf_op jit(solution)/shard_map/ppermute | solution.py:466
  70.4 1.5 %shard_map.87 = (f32[32,2048]{1,0:T(8,128)S(1)}, f32[32,2048]{1,0:T(8,128)S(1)}, f32[32,2048]{1,0:T(8,128)S(1)}, f32[32,2048]{1,0:T(8,128)S(1)}, f32[80,128]{1,0...) custom-call(s32[1]{0:T(128)S(6)} %select_n.15.core_ref.refs_0_, ...), custom_call_target="tpu_custom_call" | custom-call | flops 1500000000 | bytes 1048576 | tf_op jit(solution)/shard_map/pallas_call | solution.py:83
  71.9 2.3 %shard_map.88 = (f32[32,384]{1,0:T(8,128)S(1)}, f32[80,128]{1,0:T(8,128)S(1)}, f32[208,128]{1,0:T(8,128)S(1)}, f32[8,128]{1,0:T(8,128)S(1)}) custom-call(s32[1]{0:T(128)S(6)} %select_n.15.core_ref.refs_0_, f32[32,2048]{1,0:T(8,128)S(1)} %get-tuple-element.174.field_ref.refs_7_.refs_8_, bf16[896,2048]{1,0:T(8,128)(2,1)S(1)} %copy-done.1, ...), custom_call_target="tpu_custom_call" | custom-call | flops 3000000000 | bytes 1048576 | tf_op jit(solution)/shard_map/pallas_call | solution.py:83
  75.6 2.9 %collective-permute-start.22 = (f32[72,128]{1,0:T(8,128)S(1)}, f32[72,128]{1,0:T(8,128)S(1)}, u32[]{:S(2)}, u32[]{:S(2)}) collective-permute-start(f32[72,128]{1,0:T(8,128)S(1)} %get-tuple-element.173.refs_1_), channel_id=1, source_target_pairs={{0,6},{1,7},{2,4},{3,5},{4,2},{5,3},{6,0},{7,1},{8,14},{9,15},{10,... | collective-permute-start | bytes 110600 | tf_op jit(solution)/shard_map/ppermute | solution.py:466
  83.9 3.0 %collective-permute-start.25 = (f32[40,128]{1,0:T(8,128)S(1)}, f32[40,128]{1,0:T(8,128)S(1)}, u32[]{:S(2)}, u32[]{:S(2)}) collective-permute-start(f32[40,128]{1,0:T(8,128)S(1)} %get-tuple-element.178.refs_1_), channel_id=1, source_target_pairs={{0,24},{1,25},{2,26},{3,27},{4,28},{5,29},{6,30},{7,31},{8,16},{9,... | collective-permute-start | bytes 61448 | tf_op jit(solution)/shard_map/ppermute | solution.py:466
  89.5 2.1 %collective-permute-done.24.refs_3_ = f32[40,128]{1,0:T(8,128)S(1)} collective-permute-done((f32[40,128]{1,0:T(8,128)S(1)}, f32[40,128]{1,0:T(8,128)S(1)}, u32[]{:S(2)}, u32[]{:S(2)}) %collective-permute-start.24) | collective-permute-done | bytes 20512 | tf_op jit(solution)/shard_map/ppermute | solution.py:466
  95.5 2.3 %shard_map.96 = (f32[32,384]{1,0:T(8,128)S(1)}, f32[80,128]{1,0:T(8,128)S(1)}, f32[208,128]{1,0:T(8,128)S(1)}) custom-call(s32[1]{0:T(128)S(6)} %select_n.15.core_ref.refs_0_, f32[32,2048]{1,0:T(8,128)S(1)} %get-tuple-element.200.field_ref.refs_9_.refs_10_, bf16[896,2048]{1,0:T(8,128)(2,1)S(1)} %copy-done.1, bf16[896,2048]{1,0:T(8,128)(2,1)S(1)} %copy-done.3), custom_call_target="tpu_custom_call" | custom-call | flops 3000000000 | bytes 1048576 | tf_op jit(solution)/shard_map/pallas_call | solution.py:83
  98.7 2.9 %collective-permute-start.28 = (f32[208,128]{1,0:T(8,128)S(1)}, f32[208,128]{1,0:T(8,128)S(1)}, u32[]{:S(2)}, u32[]{:S(2)}) collective-permute-start(f32[208,128]{1,0:T(8,128)S(1)} %get-tuple-element.201), channel_id=1, source_target_pairs={{0,1},{1,0},{2,3},{3,2},{4,5},{5,4},{6,7},{7,6},{8,9},{9,8},{10,11... | collective-permute-start | bytes 319496 | tf_op jit(solution)/shard_map/ppermute | solution.py:466
  104.1 2.0 %collective-permute-start.32 = (f32[80,128]{1,0:T(8,128)S(1)}, f32[80,128]{1,0:T(8,128)S(1)}, u32[]{:S(2)}, u32[]{:S(2)}) collective-permute-start(f32[80,128]{1,0:T(8,128)S(1)} %get-tuple-element.211.refs_1_), channel_id=1, source_target_pairs={{0,6},{1,7},{2,4},{3,5},{4,2},{5,3},{6,0},{7,1},{8,14},{9,15},{10,... | collective-permute-start | bytes 122888 | tf_op jit(solution)/shard_map/ppermute | solution.py:466
  111.8 1.9 %collective-permute-start.35 = (f32[48,128]{1,0:T(8,128)S(1)}, f32[48,128]{1,0:T(8,128)S(1)}, u32[]{:S(2)}, u32[]{:S(2)}) collective-permute-start(f32[48,128]{1,0:T(8,128)S(1)} %get-tuple-element.213.refs_1_), channel_id=1, source_target_pairs={{0,24},{1,25},{2,26},{3,27},{4,28},{5,29},{6,30},{7,31},{8,16},{9,... | collective-permute-start | bytes 73736 | tf_op jit(solution)/shard_map/ppermute | solution.py:466
  114.5 1.8 %collective-permute-start.33 = (f32[48,128]{1,0:T(8,128)S(1)}, f32[48,128]{1,0:T(8,128)S(1)}, u32[]{:S(2)}, u32[]{:S(2)}) collective-permute-start(f32[48,128]{1,0:T(8,128)S(1)} %get-tuple-element.213.refs_1_), channel_id=1, source_target_pairs={{0,8},{1,9},{2,10},{3,11},{4,12},{5,13},{6,14},{7,15},{8,0},{9,1},... | collective-permute-start | bytes 73736 | tf_op jit(solution)/shard_map/ppermute | solution.py:466
  120.0 2.2 %shard_map.103 = (f32[32,2048]{1,0:T(8,128)}, f32[32,2048]{1,0:T(8,128)}) custom-call(s32[1]{0:T(128)S(6)} %select_n.15.core_ref.refs_0_, bf16[896,2048]{1,0:T(8,128)(2,1)S(1)} %copy-done.1, bf16[896,2048]{1,0:T(8,128)(2,1)S(1)} %copy-done.3, f32[32,2048]{1,0:T(8,128)S(1)} %get-tuple-element.207.refs_3_, f32[96,128]{1,0:T(8,128)S(1)} %shard_map.102.refs_4_, ...), custom_call_target="tpu_custom_call" | custom-call | flops 1500000000 | bytes 1048576 | tf_op jit(solution)/shard_map/pallas_call | solution.py:83
  (119 shorter events, 51.0 us)
Async XLA Ops:
  2.4 31.8 %collective-permute-start.8 = (f32[8,512]{1,0:T(8,128)S(1)}, f32[8,512]{1,0:T(8,128)S(1)}, u32[]{:S(2)}, u32[]{:S(2)}) collective-permute-start(f32[8,512]{1,0:T(8,128)S(1)} %get-tuple-element.129), channel_id=1, source_target_pairs={{0,1},{1,0},{2,3},{3,2},{4,5},{5,4},{6,7},{7,6},{8,9},{9,8},{10,11... | collective-permute-start | bytes 49160 | tf_op jit(solution)/shard_map/ppermute | solution.py:466
  2.9 31.3 %collective-permute-start.1 = (f32[40,512]{1,0:T(8,128)S(1)}, f32[40,512]{1,0:T(8,128)S(1)}, u32[]{:S(2)}, u32[]{:S(2)}) collective-permute-start(f32[40,512]{1,0:T(8,128)S(1)} %get-tuple-element.114), channel_id=1, source_target_pairs={{1,2},{3,4},{5,6},{7,8},{9,10},{11,12},{13,14},{15,16},{17,18},{19... | collective-permute-start | bytes 245768 | tf_op jit(solution)/shard_map/ppermute | solution.py:471
  12.4 4.8 %collective-permute-start = (f32[208,128]{1,0:T(8,128)S(1)}, f32[208,128]{1,0:T(8,128)S(1)}, u32[]{:S(2)}, u32[]{:S(2)}) collective-permute-start(f32[208,128]{1,0:T(8,128)S(1)} %get-tuple-element.113), channel_id=1, source_target_pairs={{0,1},{1,0},{2,3},{3,2},{4,5},{5,4},{6,7},{7,6},{8,9},{9,8},{10,11... | collective-permute-start | bytes 319496 | tf_op jit(solution)/shard_map/ppermute | solution.py:466
  17.2 11.4 %collective-permute-start.4 = (f32[72,128]{1,0:T(8,128)S(1)}, f32[72,128]{1,0:T(8,128)S(1)}, u32[]{:S(2)}, u32[]{:S(2)}) collective-permute-start(f32[72,128]{1,0:T(8,128)S(1)} %get-tuple-element.117.refs_1_), channel_id=1, source_target_pairs={{0,6},{1,7},{2,4},{3,5},{4,2},{5,3},{6,0},{7,1},{8,14},{9,15},{10,... | collective-permute-start | bytes 110600 | tf_op jit(solution)/shard_map/ppermute | solution.py:466
  19.7 9.0 %collective-permute-start.3 = (f32[72,128]{1,0:T(8,128)S(1)}, f32[72,128]{1,0:T(8,128)S(1)}, u32[]{:S(2)}, u32[]{:S(2)}) collective-permute-start(f32[72,128]{1,0:T(8,128)S(1)} %get-tuple-element.117.refs_1_), channel_id=1, source_target_pairs={{0,4},{1,5},{2,6},{3,7},{4,0},{5,1},{6,2},{7,3},{8,12},{9,13},{10,... | collective-permute-start | bytes 110600 | tf_op jit(solution)/shard_map/ppermute | solution.py:466
  20.2 8.5 %collective-permute-start.2 = (f32[72,128]{1,0:T(8,128)S(1)}, f32[72,128]{1,0:T(8,128)S(1)}, u32[]{:S(2)}, u32[]{:S(2)}) collective-permute-start(f32[72,128]{1,0:T(8,128)S(1)} %get-tuple-element.117.refs_1_), channel_id=1, source_target_pairs={{0,2},{1,3},{2,0},{3,1},{4,6},{5,7},{6,4},{7,5},{8,10},{9,11},{10,... | collective-permute-start | bytes 110600 | tf_op jit(solution)/shard_map/ppermute | solution.py:466
  28.7 10.7 %collective-permute-start.7 = (f32[40,128]{1,0:T(8,128)S(1)}, f32[40,128]{1,0:T(8,128)S(1)}, u32[]{:S(2)}, u32[]{:S(2)}) collective-permute-start(f32[40,128]{1,0:T(8,128)S(1)} %get-tuple-element.128.refs_1_), channel_id=1, source_target_pairs={{0,24},{1,25},{2,26},{3,27},{4,28},{5,29},{6,30},{7,31},{8,16},{9,... | collective-permute-start | bytes 61448 | tf_op jit(solution)/shard_map/ppermute | solution.py:466
  33.5 5.9 %collective-permute-start.6 = (f32[40,128]{1,0:T(8,128)S(1)}, f32[40,128]{1,0:T(8,128)S(1)}, u32[]{:S(2)}, u32[]{:S(2)}) collective-permute-start(f32[40,128]{1,0:T(8,128)S(1)} %get-tuple-element.128.refs_1_), channel_id=1, source_target_pairs={{0,16},{1,17},{2,18},{3,19},{4,20},{5,21},{6,22},{7,23},{8,24},{9,... | collective-permute-start | bytes 61448 | tf_op jit(solution)/shard_map/ppermute | solution.py:466
  33.5 5.9 %collective-permute-start.5 = (f32[40,128]{1,0:T(8,128)S(1)}, f32[40,128]{1,0:T(8,128)S(1)}, u32[]{:S(2)}, u32[]{:S(2)}) collective-permute-start(f32[40,128]{1,0:T(8,128)S(1)} %get-tuple-element.128.refs_1_), channel_id=1, source_target_pairs={{0,8},{1,9},{2,10},{3,11},{4,12},{5,13},{6,14},{7,15},{8,0},{9,1},... | collective-permute-start | bytes 61448 | tf_op jit(solution)/shard_map/ppermute | solution.py:466
  51.3 5.6 %collective-permute-start.14 = (f32[80,128]{1,0:T(8,128)S(1)}, f32[80,128]{1,0:T(8,128)S(1)}, u32[]{:S(2)}, u32[]{:S(2)}) collective-permute-start(f32[80,128]{1,0:T(8,128)S(1)} %get-tuple-element.158.refs_1_), channel_id=1, source_target_pairs={{0,6},{1,7},{2,4},{3,5},{4,2},{5,3},{6,0},{7,1},{8,14},{9,15},{10,... | collective-permute-start | bytes 122888 | tf_op jit(solution)/shard_map/ppermute | solution.py:466
  55.0 4.2 %collective-permute-start.12 = (f32[80,128]{1,0:T(8,128)S(1)}, f32[80,128]{1,0:T(8,128)S(1)}, u32[]{:S(2)}, u32[]{:S(2)}) collective-permute-start(f32[80,128]{1,0:T(8,128)S(1)} %get-tuple-element.158.refs_1_), channel_id=1, source_target_pairs={{0,2},{1,3},{2,0},{3,1},{4,6},{5,7},{6,4},{7,5},{8,10},{9,11},{10,... | collective-permute-start | bytes 122888 | tf_op jit(solution)/shard_map/ppermute | solution.py:466
  59.4 6.5 %collective-permute-start.17 = (f32[48,128]{1,0:T(8,128)S(1)}, f32[48,128]{1,0:T(8,128)S(1)}, u32[]{:S(2)}, u32[]{:S(2)}) collective-permute-start(f32[48,128]{1,0:T(8,128)S(1)} %get-tuple-element.160.refs_1_), channel_id=1, source_target_pairs={{0,24},{1,25},{2,26},{3,27},{4,28},{5,29},{6,30},{7,31},{8,16},{9,... | collective-permute-start | bytes 73736 | tf_op jit(solution)/shard_map/ppermute | solution.py:466
  64.2 4.7 %collective-permute-start.16 = (f32[48,128]{1,0:T(8,128)S(1)}, f32[48,128]{1,0:T(8,128)S(1)}, u32[]{:S(2)}, u32[]{:S(2)}) collective-permute-start(f32[48,128]{1,0:T(8,128)S(1)} %get-tuple-element.160.refs_1_), channel_id=1, source_target_pairs={{0,16},{1,17},{2,18},{3,19},{4,20},{5,21},{6,22},{7,23},{8,24},{9,... | collective-permute-start | bytes 73736 | tf_op jit(solution)/shard_map/ppermute | solution.py:466
  64.2 4.7 %collective-permute-start.15 = (f32[48,128]{1,0:T(8,128)S(1)}, f32[48,128]{1,0:T(8,128)S(1)}, u32[]{:S(2)}, u32[]{:S(2)}) collective-permute-start(f32[48,128]{1,0:T(8,128)S(1)} %get-tuple-element.160.refs_1_), channel_id=1, source_target_pairs={{0,8},{1,9},{2,10},{3,11},{4,12},{5,13},{6,14},{7,15},{8,0},{9,1},... | collective-permute-start | bytes 73736 | tf_op jit(solution)/shard_map/ppermute | solution.py:466
  74.4 13.9 %collective-permute-start.26 = (f32[32,512]{1,0:T(8,128)S(1)}, f32[32,512]{1,0:T(8,128)S(1)}, u32[]{:S(2)}, u32[]{:S(2)}) collective-permute-start(f32[32,512]{1,0:T(8,128)S(1)} %get-tuple-element.179), channel_id=1, source_target_pairs={{1,2},{3,4},{5,6},{7,8},{9,10},{11,12},{13,14},{15,16},{17,18},{19... | collective-permute-start | bytes 196616 | tf_op jit(solution)/shard_map/ppermute | solution.py:471
  75.6 8.1 %collective-permute-start.22 = (f32[72,128]{1,0:T(8,128)S(1)}, f32[72,128]{1,0:T(8,128)S(1)}, u32[]{:S(2)}, u32[]{:S(2)}) collective-permute-start(f32[72,128]{1,0:T(8,128)S(1)} %get-tuple-element.173.refs_1_), channel_id=1, source_target_pairs={{0,6},{1,7},{2,4},{3,5},{4,2},{5,3},{6,0},{7,1},{8,14},{9,15},{10,... | collective-permute-start | bytes 110600 | tf_op jit(solution)/shard_map/ppermute | solution.py:466
  78.5 5.3 %collective-permute-start.21 = (f32[72,128]{1,0:T(8,128)S(1)}, f32[72,128]{1,0:T(8,128)S(1)}, u32[]{:S(2)}, u32[]{:S(2)}) collective-permute-start(f32[72,128]{1,0:T(8,128)S(1)} %get-tuple-element.173.refs_1_), channel_id=1, source_target_pairs={{0,4},{1,5},{2,6},{3,7},{4,0},{5,1},{6,2},{7,3},{8,12},{9,13},{10,... | collective-permute-start | bytes 110600 | tf_op jit(solution)/shard_map/ppermute | solution.py:466
  83.9 5.6 %collective-permute-start.25 = (f32[40,128]{1,0:T(8,128)S(1)}, f32[40,128]{1,0:T(8,128)S(1)}, u32[]{:S(2)}, u32[]{:S(2)}) collective-permute-start(f32[40,128]{1,0:T(8,128)S(1)} %get-tuple-element.178.refs_1_), channel_id=1, source_target_pairs={{0,24},{1,25},{2,26},{3,27},{4,28},{5,29},{6,30},{7,31},{8,16},{9,... | collective-permute-start | bytes 61448 | tf_op jit(solution)/shard_map/ppermute | solution.py:466
  86.9 4.7 %collective-permute-start.24 = (f32[40,128]{1,0:T(8,128)S(1)}, f32[40,128]{1,0:T(8,128)S(1)}, u32[]{:S(2)}, u32[]{:S(2)}) collective-permute-start(f32[40,128]{1,0:T(8,128)S(1)} %get-tuple-element.178.refs_1_), channel_id=1, source_target_pairs={{0,16},{1,17},{2,18},{3,19},{4,20},{5,21},{6,22},{7,23},{8,24},{9,... | collective-permute-start | bytes 61448 | tf_op jit(solution)/shard_map/ppermute | solution.py:466
  86.9 4.7 %collective-permute-start.23 = (f32[40,128]{1,0:T(8,128)S(1)}, f32[40,128]{1,0:T(8,128)S(1)}, u32[]{:S(2)}, u32[]{:S(2)}) collective-permute-start(f32[40,128]{1,0:T(8,128)S(1)} %get-tuple-element.178.refs_1_), channel_id=1, source_target_pairs={{0,8},{1,9},{2,10},{3,11},{4,12},{5,13},{6,14},{7,15},{8,0},{9,1},... | collective-permute-start | bytes 61448 | tf_op jit(solution)/shard_map/ppermute | solution.py:466
  97.8 5.1 %collective-permute-start.29 = (f32[32,512]{1,0:T(8,128)S(1)}, f32[32,512]{1,0:T(8,128)S(1)}, u32[]{:S(2)}, u32[]{:S(2)}) collective-permute-start(f32[32,512]{1,0:T(8,128)S(1)} %get-tuple-element.202), channel_id=1, source_target_pairs={{1,2},{3,4},{5,6},{7,8},{9,10},{11,12},{13,14},{15,16},{17,18},{19... | collective-permute-start | bytes 196616 | tf_op jit(solution)/shard_map/ppermute | solution.py:471
  104.1 5.1 %collective-permute-start.32 = (f32[80,128]{1,0:T(8,128)S(1)}, f32[80,128]{1,0:T(8,128)S(1)}, u32[]{:S(2)}, u32[]{:S(2)}) collective-permute-start(f32[80,128]{1,0:T(8,128)S(1)} %get-tuple-element.211.refs_1_), channel_id=1, source_target_pairs={{0,6},{1,7},{2,4},{3,5},{4,2},{5,3},{6,0},{7,1},{8,14},{9,15},{10,... | collective-permute-start | bytes 122888 | tf_op jit(solution)/shard_map/ppermute | solution.py:466
  111.8 5.6 %collective-permute-start.35 = (f32[48,128]{1,0:T(8,128)S(1)}, f32[48,128]{1,0:T(8,128)S(1)}, u32[]{:S(2)}, u32[]{:S(2)}) collective-permute-start(f32[48,128]{1,0:T(8,128)S(1)} %get-tuple-element.213.refs_1_), channel_id=1, source_target_pairs={{0,24},{1,25},{2,26},{3,27},{4,28},{5,29},{6,30},{7,31},{8,16},{9,... | collective-permute-start | bytes 73736 | tf_op jit(solution)/shard_map/ppermute | solution.py:466
  113.7 4.8 %collective-permute-start.34 = (f32[48,128]{1,0:T(8,128)S(1)}, f32[48,128]{1,0:T(8,128)S(1)}, u32[]{:S(2)}, u32[]{:S(2)}) collective-permute-start(f32[48,128]{1,0:T(8,128)S(1)} %get-tuple-element.213.refs_1_), channel_id=1, source_target_pairs={{0,16},{1,17},{2,18},{3,19},{4,20},{5,21},{6,22},{7,23},{8,24},{9,... | collective-permute-start | bytes 73736 | tf_op jit(solution)/shard_map/ppermute | solution.py:466
  (26 other events, 98.0 us)
where the time goes:
time: 123 us; the launch traced here: 122 us
  starting transfers between devices  50.6 us (41%)
  Pallas kernels  44.5 us (36%)
  waiting for transfers between devices  20.8 us (17%)
  local copies, waits for them, and re-layouts  5.05 us (4%)
    ppermute x33, starting transfers between devices, swap(): lax.ppermute(value, BOTH, [(source, source ^ mask) for source in range(de...  47.4 us
    pallas_call x35, Pallas kernels, call(): pl.pallas_call(body, out_shape=outs, in_specs=[whole(pltpu.SMEM)] * scala...  39.5 us
    ppermute x33, waiting for transfers between devices, swap(): lax.ppermute(value, BOTH, [(source, source ^ mask) for source in range(de...  20.7 us
    pallas_call x1, Pallas kernels, per_device(): pl.pallas_call(functools.partial(setup_kernel, pairs), out_shape=[bf16(ha...  5.01 us
    unnamed x26, local copies, waits for them, and re-layouts  4.8 us
    ppermute x4, starting transfers between devices, halo(): lax.ppermute(other, BOTH, outward + [(target, source) for source, target...  3.19 us
  transfers between devices with their start and end apart: 37, of which 19 were waited for; matrix products, arithmetic and copies ran while one was open for 0% of the time, Pallas kernels for 21%

commit v1 on v0

--- a/solution.py
+++ b/solution.py
@@ -16,7 +16,7 @@
 CHUNK = 16
 NORM_TILE = 8
 PRODUCTS_TILE = 16
-FLOPS = 3 * 10**9
+FLOPS = 0
 
 root_three = 1.7320508075688772
 spacing_factor = 1.6
@@ -103,7 +103,6 @@
     for axis in range(3):
         spread = rows[:, axis : axis + 1] - lanes[axis : axis + 1]
         square = spread * spread if square is None else square + spread * spread
-    square = square * (matern_scale * matern_scale)
     scaled = square * lax.rsqrt(jnp.maximum(square, 1e-30))
     return halves((1.0 + scaled) * jnp.exp(-scaled))
 
@@ -457,6 +456,7 @@
     place = jnp.reshape(lax.axis_index(BOTH), (1,))
     core = place % 2
     nugget = nugget[None, :]
+    coords = coords * matern_scale
     weights = leaf_weights(near_ids, place[0] * leaves)
 
     stages = [list(range(bit, min(bit + 2, crossing))) for bit in range(1, crossing, 2)]
@@ -538,7 +538,7 @@
         functools.partial(setup_kernel, pairs),
         out_shape=[bf16(half, LEAF, LEAF)] * 2
         + [pltpu.VMEM((levels * LANES, width), jnp.bfloat16)] * 2
-        + [f32(width, 8)],
+        + [pltpu.VMEM((width, 8), jnp.float32)],
         in_specs=[whole(), whole(pltpu.HBM)],
         out_specs=[whole()] * 5,
         scratch_shapes=[pltpu.VMEM(basis.shape, jnp.float32), pltpu.SemaphoreType.DMA((levels,))],

time: 123 us -> 133 us (1.081)
  local copies, waits for them, and re-layouts: 5.05 us -> 13 us
  Pallas kernels: 44.5 us -> 47.9 us
  starting transfers between devices: 50.6 us -> 49 us
    unnamed x26 -> x52, local copies, waits for them, and re-layouts: 4.8 us -> 12.7 us
    pallas_call x35, Pallas kernels: 39.5 us -> 43 us  [call(): pl.pallas_call(body, out_shape=outs, in_specs=[whole(pltpu.SMEM)] * scala...]
    ppermute x33, starting transfers between devices: 47.4 us -> 44.4 us  [swap(): lax.ppermute(value, BOTH, [(source, source ^ mask) for source in range(de...]
    ppermute x4, starting transfers between devices: 3.19 us -> 4.62 us  [halo(): lax.ppermute(other, BOTH, outward + [(target, source) for source, target...]
  transfers between devices with their start and end apart: 37 -> 37, of which waited for: 19 -> 17; matrix products, arithmetic and copies ran while one was open for 0% -> 0% of each run, Pallas kernels for 21% -> 22%
where the time goes in v1:
time: 133 us
  starting transfers between devices  49 us (37%)
  Pallas kernels  47.9 us (36%)
  waiting for transfers between devices  20.8 us (16%)
  local copies, waits for them, and re-layouts  13 us (10%)
    ppermute x33, starting transfers between devices, swap(): lax.ppermute(value, BOTH, [(source, source ^ mask) for source in range(de...  44.4 us
    pallas_call x35, Pallas kernels, call(): pl.pallas_call(body, out_shape=outs, in_specs=[whole(pltpu.SMEM)] * scala...  43 us
    ppermute x33, waiting for transfers between devices, swap(): lax.ppermute(value, BOTH, [(source, source ^ mask) for source in range(de...  20.8 us
    unnamed x52, local copies, waits for them, and re-layouts  12.7 us
    pallas_call x1, Pallas kernels, per_device(): pl.pallas_call(functools.partial(setup_kernel, pairs), out_shape=[bf16(ha...  4.87 us
    ppermute x4, starting transfers between devices, halo(): lax.ppermute(other, BOTH, outward + [(target, source) for source, target...  4.62 us
  transfers between devices with their start and end apart: 37, of which 17 were waited for; matrix products, arithmetic and copies ran while one was open for 0% of the time, Pallas kernels for 22%

profile of v1, /device:TPU:0, one launch (start us, length us, event | category | flops | bytes accessed | tf_op | source)
XLA Modules:
  0.0 132.8 jit_solution(11596445274306796673)
XLA Ops:
  3.5 2.3 %collective-permute-start.1 = (f32[40,512]{1,0:T(8,128)}, f32[40,512]{1,0:T(8,128)}, u32[]{:S(2)}, u32[]{:S(2)}) collective-permute-start(f32[40,512]{1,0:T(8,128)} %get-tuple-element.114), channel_id=1, source_target_pairs={{1,2},{3,4},{5,6},{7,8},{9,10},{11,12},{13,14},{15,16},{17,18},{19... | collective-permute-start | bytes 245768 | tf_op jit(solution)/shard_map/ppermute | solution.py:471
  5.7 4.9 %shard_map.68 = (bf16[2,512,512]{2,1,0:T(8,128)(2,1)S(1)}, bf16[2,512,512]{2,1,0:T(8,128)(2,1)}, bf16[896,2048]{1,0:T(8,128)(2,1)S(1)}, bf16[896,2048]{1,0:T(8,128)(2,1)S(1)}, f32[2048,8]{1,0:T(8,128)S(1)}) custom-call(f32[3,2048]{1,0:T(4,128)S(1)} %broadcast_multiply_fusion.lane_ref.coords_ref, f32[7,128,2048]{2,1,0:T(8,128)} %basis_ref.1), custom_call_target="tpu_custom_call" | custom-call | bytes 1048576 | tf_op jit(solution)/shard_map/pallas_call | solution.py:537
  12.7 2.3 %shard_map.69 = (f32[32,384]{1,0:T(8,128)S(1)}, f32[80,128]{1,0:T(8,128)S(1)}, f32[208,128]{1,0:T(8,128)S(1)}, f32[8,128]{1,0:T(8,128)S(1)}) custom-call(s32[1]{0:T(128)S(6)} %select_n.15.core_ref.refs_0_, f32[32,2048]{1,0:T(8,128)S(1)} %copy-done.18, bf16[896,2048]{1,0:T(8,128)(2,1)S(1)} %get-tuple-element.111.high_ref.refs_1_, ...), custom_call_target="tpu_custom_call" | custom-call | bytes 1048576 | tf_op jit(solution)/shard_map/pallas_call | solution.py:83
  15.6 2.4 %collective-permute-start = (f32[208,128]{1,0:T(8,128)S(1)}, f32[208,128]{1,0:T(8,128)S(1)}, u32[]{:S(2)}, u32[]{:S(2)}) collective-permute-start(f32[208,128]{1,0:T(8,128)S(1)} %get-tuple-element.113), channel_id=1, source_target_pairs={{0,1},{1,0},{2,3},{3,2},{4,5},{5,4},{6,7},{7,6},{8,9},{9,8},{10,11... | collective-permute-start | bytes 319496 | tf_op jit(solution)/shard_map/ppermute | solution.py:466
  18.9 2.5 %collective-permute-start.4 = (f32[72,128]{1,0:T(8,128)S(1)}, f32[72,128]{1,0:T(8,128)S(1)}, u32[]{:S(2)}, u32[]{:S(2)}) collective-permute-start(f32[72,128]{1,0:T(8,128)S(1)} %get-tuple-element.117.refs_1_), channel_id=1, source_target_pairs={{0,6},{1,7},{2,4},{3,5},{4,2},{5,3},{6,0},{7,1},{8,14},{9,15},{10,... | collective-permute-start | bytes 110600 | tf_op jit(solution)/shard_map/ppermute | solution.py:466
  23.7 6.5 %shard_map.72 = (bf16[2,512,512]{2,1,0:T(8,128)(2,1)S(1)}, bf16[2,512,512]{2,1,0:T(8,128)(2,1)S(1)}, bf16[3,512,512]{2,1,0:T(8,128)(2,1)S(1)}, bf16[3,512,512]{2,1,0:T(8,128)(2,1)S(1)}) custom-call(f32[3,2048]{1,0:T(4,128)S(1)} %broadcast_multiply_fusion.lane_ref.coords_ref, f32[2048,8]{1,0:T(8,128)S(1)} %copy-done.20), custom_call_target="tpu_custom_call" | custom-call | bytes 1048576 | tf_op jit(solution)/shard_map/pallas_call | solution.py:83
  32.3 4.8 %collective-permute-start.7 = (f32[40,128]{1,0:T(8,128)S(1)}, f32[40,128]{1,0:T(8,128)S(1)}, u32[]{:S(2)}, u32[]{:S(2)}) collective-permute-start(f32[40,128]{1,0:T(8,128)S(1)} %get-tuple-element.128.refs_1_), channel_id=1, source_target_pairs={{0,24},{1,25},{2,26},{3,27},{4,28},{5,29},{6,30},{7,31},{8,16},{9,... | collective-permute-start | bytes 61448 | tf_op jit(solution)/shard_map/ppermute | solution.py:466
  39.3 3.5 %shard_map.74 = (bf16[2,512,512]{2,1,0:T(8,128)(2,1)S(1)}, bf16[2,512,512]{2,1,0:T(8,128)(2,1)S(1)}) custom-call(s32[1]{0:T(128)S(6)} %select_n.15.core_ref.refs_0_, f32[2048,8]{1,0:T(8,128)S(1)} %copy-done.21, f32[8,512]{1,0:T(8,128)S(1)} %collective-permute-done.8.refs_1_, f32[40,512]{1,0:T(8,128)} %collective-permute-done.1.refs_2_.refs_3_), custom_call_target="tpu_custom_call" | custom-call | bytes 1048576 | tf_op jit(solution)/shard_map/pallas_call | solution.py:83
  50.3 2.2 %shard_map.77.refs_3_ = f32[32,2048]{1,0:T(8,128)S(1)} custom-call(s32[1]{0:T(128)S(6)} %select_n.15.core_ref.refs_0_, f32[12,512]{1,0:T(8,128)S(1)} %broadcast_in_dim.22.weights_ref.refs_1_, f32[208,128]{1,0:T(8,128)S(1)} %copy-done.24, f32[40,512]{1,0:T(8,128)} %collective-permute-done.1.refs_2_.refs_3_, bf16[2,512,512]{2,1,0:T(8,128)(2,1)S(1)} %copy-done.5, ...), custom_call_target="tpu_custom_call" | custom-call | bytes 1048576 | tf_op jit(solution)/shard_map/pallas_call | solution.py:83
  52.5 2.2 %shard_map.79 = (f32[32,2048]{1,0:T(8,128)S(1)}, f32[32,128]{1,0:T(8,128)S(1)}, f32[32,512]{1,0:T(8,128)S(1)}) custom-call(s32[1]{0:T(128)S(6)} %select_n.15.core_ref.refs_0_, bf16[896,2048]{1,0:T(8,128)(2,1)S(1)} %copy-done.1, bf16[896,2048]{1,0:T(8,128)(2,1)S(1)} %copy-done.3, f32[32,2048]{1,0:T(8,128)S(1)} %shard_map.77.refs_3_, ...), custom_call_target="tpu_custom_call" | custom-call | bytes 1048576 | tf_op jit(solution)/shard_map/pallas_call | solution.py:83
  54.7 2.3 %shard_map.80 = (f32[32,384]{1,0:T(8,128)S(1)}, f32[80,128]{1,0:T(8,128)S(1)}, f32[208,128]{1,0:T(8,128)S(1)}) custom-call(s32[1]{0:T(128)S(6)} %select_n.15.core_ref.refs_0_, f32[32,2048]{1,0:T(8,128)S(1)} %get-tuple-element.151.field_ref.refs_9_.refs_11_.refs_8_.refs_10_, bf16[896,2048]{1,0:T(8,128)(2,1)S(1)} %copy-done.1, bf16[896,2048]{1,0:T(8,128)(2,1)S(1)} %copy-done.3), custom_call_target="tpu_custom_call" | custom-call | bytes 1048576 | tf_op jit(solution)/shard_map/pallas_call | solution.py:83
  62.1 4.2 %collective-permute-start.14 = (f32[80,128]{1,0:T(8,128)S(1)}, f32[80,128]{1,0:T(8,128)S(1)}, u32[]{:S(2)}, u32[]{:S(2)}) collective-permute-start(f32[80,128]{1,0:T(8,128)S(1)} %get-tuple-element.158.refs_1_), channel_id=1, source_target_pairs={{0,6},{1,7},{2,4},{3,5},{4,2},{5,3},{6,0},{7,1},{8,14},{9,15},{10,... | collective-permute-start | bytes 122888 | tf_op jit(solution)/shard_map/ppermute | solution.py:466
  68.3 2.4 %collective-permute-done.13.refs_3_ = f32[80,128]{1,0:T(8,128)S(1)} collective-permute-done((f32[80,128]{1,0:T(8,128)S(1)}, f32[80,128]{1,0:T(8,128)S(1)}, u32[]{:S(2)}, u32[]{:S(2)}) %collective-permute-start.13) | collective-permute-done | bytes 40992 | tf_op jit(solution)/shard_map/ppermute | solution.py:466
  71.3 4.4 %collective-permute-start.17 = (f32[48,128]{1,0:T(8,128)S(1)}, f32[48,128]{1,0:T(8,128)S(1)}, u32[]{:S(2)}, u32[]{:S(2)}) collective-permute-start(f32[48,128]{1,0:T(8,128)S(1)} %get-tuple-element.160.refs_1_), channel_id=1, source_target_pairs={{0,24},{1,25},{2,26},{3,27},{4,28},{5,29},{6,30},{7,31},{8,16},{9,... | collective-permute-start | bytes 73736 | tf_op jit(solution)/shard_map/ppermute | solution.py:466
  77.4 2.9 %collective-permute-done.16.refs_3_ = f32[48,128]{1,0:T(8,128)S(1)} collective-permute-done((f32[48,128]{1,0:T(8,128)S(1)}, f32[48,128]{1,0:T(8,128)S(1)}, u32[]{:S(2)}, u32[]{:S(2)}) %collective-permute-start.16) | collective-permute-done | bytes 24608 | tf_op jit(solution)/shard_map/ppermute | solution.py:466
  83.3 2.3 %shard_map.88 = (f32[32,384]{1,0:T(8,128)S(1)}, f32[80,128]{1,0:T(8,128)S(1)}, f32[208,128]{1,0:T(8,128)S(1)}, f32[8,128]{1,0:T(8,128)S(1)}) custom-call(s32[1]{0:T(128)S(6)} %select_n.15.core_ref.refs_0_, f32[32,2048]{1,0:T(8,128)S(1)} %get-tuple-element.174.field_ref.refs_7_.refs_8_, bf16[896,2048]{1,0:T(8,128)(2,1)S(1)} %copy-done.1, ...), custom_call_target="tpu_custom_call" | custom-call | bytes 1048576 | tf_op jit(solution)/shard_map/pallas_call | solution.py:83
  87.0 2.9 %collective-permute-start.22 = (f32[72,128]{1,0:T(8,128)S(1)}, f32[72,128]{1,0:T(8,128)S(1)}, u32[]{:S(2)}, u32[]{:S(2)}) collective-permute-start(f32[72,128]{1,0:T(8,128)S(1)} %get-tuple-element.173.refs_1_), channel_id=1, source_target_pairs={{0,6},{1,7},{2,4},{3,5},{4,2},{5,3},{6,0},{7,1},{8,14},{9,15},{10,... | collective-permute-start | bytes 110600 | tf_op jit(solution)/shard_map/ppermute | solution.py:466
  95.3 3.2 %collective-permute-start.25 = (f32[40,128]{1,0:T(8,128)S(1)}, f32[40,128]{1,0:T(8,128)S(1)}, u32[]{:S(2)}, u32[]{:S(2)}) collective-permute-start(f32[40,128]{1,0:T(8,128)S(1)} %get-tuple-element.178.refs_1_), channel_id=1, source_target_pairs={{0,24},{1,25},{2,26},{3,27},{4,28},{5,29},{6,30},{7,31},{8,16},{9,... | collective-permute-start | bytes 61448 | tf_op jit(solution)/shard_map/ppermute | solution.py:466
  101.0 2.2 %collective-permute-done.24.refs_3_ = f32[40,128]{1,0:T(8,128)S(1)} collective-permute-done((f32[40,128]{1,0:T(8,128)S(1)}, f32[40,128]{1,0:T(8,128)S(1)}, u32[]{:S(2)}, u32[]{:S(2)}) %collective-permute-start.24) | collective-permute-done | bytes 20512 | tf_op jit(solution)/shard_map/ppermute | solution.py:466
  105.9 2.3 %shard_map.96 = (f32[32,384]{1,0:T(8,128)S(1)}, f32[80,128]{1,0:T(8,128)S(1)}, f32[208,128]{1,0:T(8,128)S(1)}) custom-call(s32[1]{0:T(128)S(6)} %select_n.15.core_ref.refs_0_, f32[32,2048]{1,0:T(8,128)S(1)} %get-tuple-element.200.field_ref.refs_9_.refs_10_, bf16[896,2048]{1,0:T(8,128)(2,1)S(1)} %copy-done.1, bf16[896,2048]{1,0:T(8,128)(2,1)S(1)} %copy-done.3), custom_call_target="tpu_custom_call" | custom-call | bytes 1048576 | tf_op jit(solution)/shard_map/pallas_call | solution.py:83
  112.9 3.7 %collective-permute-start.32 = (f32[80,128]{1,0:T(8,128)S(1)}, f32[80,128]{1,0:T(8,128)S(1)}, u32[]{:S(2)}, u32[]{:S(2)}) collective-permute-start(f32[80,128]{1,0:T(8,128)S(1)} %get-tuple-element.211.refs_1_), channel_id=1, source_target_pairs={{0,6},{1,7},{2,4},{3,5},{4,2},{5,3},{6,0},{7,1},{8,14},{9,15},{10,... | collective-permute-start | bytes 122888 | tf_op jit(solution)/shard_map/ppermute | solution.py:466
  118.6 2.0 %collective-permute-done.31.refs_3_ = f32[80,128]{1,0:T(8,128)S(1)} collective-permute-done((f32[80,128]{1,0:T(8,128)S(1)}, f32[80,128]{1,0:T(8,128)S(1)}, u32[]{:S(2)}, u32[]{:S(2)}) %collective-permute-start.31) | collective-permute-done | bytes 40992 | tf_op jit(solution)/shard_map/ppermute | solution.py:466
  125.0 1.9 %collective-permute-start.33 = (f32[48,128]{1,0:T(8,128)S(1)}, f32[48,128]{1,0:T(8,128)S(1)}, u32[]{:S(2)}, u32[]{:S(2)}) collective-permute-start(f32[48,128]{1,0:T(8,128)S(1)} %get-tuple-element.213.refs_1_), channel_id=1, source_target_pairs={{0,8},{1,9},{2,10},{3,11},{4,12},{5,13},{6,14},{7,15},{8,0},{9,1},... | collective-permute-start | bytes 73736 | tf_op jit(solution)/shard_map/ppermute | solution.py:466
  130.6 2.2 %shard_map.103 = (f32[32,2048]{1,0:T(8,128)}, f32[32,2048]{1,0:T(8,128)}) custom-call(s32[1]{0:T(128)S(6)} %select_n.15.core_ref.refs_0_, bf16[896,2048]{1,0:T(8,128)(2,1)S(1)} %copy-done.1, bf16[896,2048]{1,0:T(8,128)(2,1)S(1)} %copy-done.3, f32[32,2048]{1,0:T(8,128)S(1)} %get-tuple-element.207.refs_3_, f32[96,128]{1,0:T(8,128)S(1)} %shard_map.102.refs_4_, ...), custom_call_target="tpu_custom_call" | custom-call | bytes 1048576 | tf_op jit(solution)/shard_map/pallas_call | solution.py:83
  (146 shorter events, 59.1 us)
Async XLA Ops:
  3.0 35.0 %collective-permute-start.8 = (f32[8,512]{1,0:T(8,128)S(1)}, f32[8,512]{1,0:T(8,128)S(1)}, u32[]{:S(2)}, u32[]{:S(2)}) collective-permute-start(f32[8,512]{1,0:T(8,128)S(1)} %get-tuple-element.129), channel_id=1, source_target_pairs={{0,1},{1,0},{2,3},{3,2},{4,5},{5,4},{6,7},{7,6},{8,9},{9,8},{10,11... | collective-permute-start | bytes 49160 | tf_op jit(solution)/shard_map/ppermute | solution.py:466
  3.5 34.6 %collective-permute-start.1 = (f32[40,512]{1,0:T(8,128)}, f32[40,512]{1,0:T(8,128)}, u32[]{:S(2)}, u32[]{:S(2)}) collective-permute-start(f32[40,512]{1,0:T(8,128)} %get-tuple-element.114), channel_id=1, source_target_pairs={{1,2},{3,4},{5,6},{7,8},{9,10},{11,12},{13,14},{15,16},{17,18},{19... | collective-permute-start | bytes 245768 | tf_op jit(solution)/shard_map/ppermute | solution.py:471
  18.9 13.4 %collective-permute-start.4 = (f32[72,128]{1,0:T(8,128)S(1)}, f32[72,128]{1,0:T(8,128)S(1)}, u32[]{:S(2)}, u32[]{:S(2)}) collective-permute-start(f32[72,128]{1,0:T(8,128)S(1)} %get-tuple-element.117.refs_1_), channel_id=1, source_target_pairs={{0,6},{1,7},{2,4},{3,5},{4,2},{5,3},{6,0},{7,1},{8,14},{9,15},{10,... | collective-permute-start | bytes 110600 | tf_op jit(solution)/shard_map/ppermute | solution.py:466
  21.4 10.9 %collective-permute-start.3 = (f32[72,128]{1,0:T(8,128)S(1)}, f32[72,128]{1,0:T(8,128)S(1)}, u32[]{:S(2)}, u32[]{:S(2)}) collective-permute-start(f32[72,128]{1,0:T(8,128)S(1)} %get-tuple-element.117.refs_1_), channel_id=1, source_target_pairs={{0,4},{1,5},{2,6},{3,7},{4,0},{5,1},{6,2},{7,3},{8,12},{9,13},{10,... | collective-permute-start | bytes 110600 | tf_op jit(solution)/shard_map/ppermute | solution.py:466
  21.9 10.4 %collective-permute-start.2 = (f32[72,128]{1,0:T(8,128)S(1)}, f32[72,128]{1,0:T(8,128)S(1)}, u32[]{:S(2)}, u32[]{:S(2)}) collective-permute-start(f32[72,128]{1,0:T(8,128)S(1)} %get-tuple-element.117.refs_1_), channel_id=1, source_target_pairs={{0,2},{1,3},{2,0},{3,1},{4,6},{5,7},{6,4},{7,5},{8,10},{9,11},{10,... | collective-permute-start | bytes 110600 | tf_op jit(solution)/shard_map/ppermute | solution.py:466
  32.3 12.5 %collective-permute-start.7 = (f32[40,128]{1,0:T(8,128)S(1)}, f32[40,128]{1,0:T(8,128)S(1)}, u32[]{:S(2)}, u32[]{:S(2)}) collective-permute-start(f32[40,128]{1,0:T(8,128)S(1)} %get-tuple-element.128.refs_1_), channel_id=1, source_target_pairs={{0,24},{1,25},{2,26},{3,27},{4,28},{5,29},{6,30},{7,31},{8,16},{9,... | collective-permute-start | bytes 61448 | tf_op jit(solution)/shard_map/ppermute | solution.py:466
  37.2 7.6 %collective-permute-start.6 = (f32[40,128]{1,0:T(8,128)S(1)}, f32[40,128]{1,0:T(8,128)S(1)}, u32[]{:S(2)}, u32[]{:S(2)}) collective-permute-start(f32[40,128]{1,0:T(8,128)S(1)} %get-tuple-element.128.refs_1_), channel_id=1, source_target_pairs={{0,16},{1,17},{2,18},{3,19},{4,20},{5,21},{6,22},{7,23},{8,24},{9,... | collective-permute-start | bytes 61448 | tf_op jit(solution)/shard_map/ppermute | solution.py:466
  37.2 7.6 %collective-permute-start.5 = (f32[40,128]{1,0:T(8,128)S(1)}, f32[40,128]{1,0:T(8,128)S(1)}, u32[]{:S(2)}, u32[]{:S(2)}) collective-permute-start(f32[40,128]{1,0:T(8,128)S(1)} %get-tuple-element.128.refs_1_), channel_id=1, source_target_pairs={{0,8},{1,9},{2,10},{3,11},{4,12},{5,13},{6,14},{7,15},{8,0},{9,1},... | collective-permute-start | bytes 61448 | tf_op jit(solution)/shard_map/ppermute | solution.py:466
  44.8 7.7 %collective-permute-start.9 = (f32[88,128]{1,0:T(8,128)S(1)}, f32[88,128]{1,0:T(8,128)}, u32[]{:S(2)}, u32[]{:S(2)}) collective-permute-start(f32[88,128]{1,0:T(8,128)S(1)} %get-tuple-element.149.refs_4_.refs_5_.refs_6_.refs_12_.refs_13_), channel_id=1, source_target_pairs={{0,1},{1,0},{2,3},{3,2},{4,5},{5,4},{6,7},{7,6},{8,9},{9,8},{10,11... | collective-permute-start | bytes 135176 | tf_op jit(solution)/shard_map/ppermute | solution.py:466
  62.1 6.2 %collective-permute-start.14 = (f32[80,128]{1,0:T(8,128)S(1)}, f32[80,128]{1,0:T(8,128)S(1)}, u32[]{:S(2)}, u32[]{:S(2)}) collective-permute-start(f32[80,128]{1,0:T(8,128)S(1)} %get-tuple-element.158.refs_1_), channel_id=1, source_target_pairs={{0,6},{1,7},{2,4},{3,5},{4,2},{5,3},{6,0},{7,1},{8,14},{9,15},{10,... | collective-permute-start | bytes 122888 | tf_op jit(solution)/shard_map/ppermute | solution.py:466
  66.3 4.4 %collective-permute-start.13 = (f32[80,128]{1,0:T(8,128)S(1)}, f32[80,128]{1,0:T(8,128)S(1)}, u32[]{:S(2)}, u32[]{:S(2)}) collective-permute-start(f32[80,128]{1,0:T(8,128)S(1)} %get-tuple-element.158.refs_1_), channel_id=1, source_target_pairs={{0,4},{1,5},{2,6},{3,7},{4,0},{5,1},{6,2},{7,3},{8,12},{9,13},{10,... | collective-permute-start | bytes 122888 | tf_op jit(solution)/shard_map/ppermute | solution.py:466
  66.8 4.2 %collective-permute-start.12 = (f32[80,128]{1,0:T(8,128)S(1)}, f32[80,128]{1,0:T(8,128)S(1)}, u32[]{:S(2)}, u32[]{:S(2)}) collective-permute-start(f32[80,128]{1,0:T(8,128)S(1)} %get-tuple-element.158.refs_1_), channel_id=1, source_target_pairs={{0,2},{1,3},{2,0},{3,1},{4,6},{5,7},{6,4},{7,5},{8,10},{9,11},{10,... | collective-permute-start | bytes 122888 | tf_op jit(solution)/shard_map/ppermute | solution.py:466
  71.3 6.2 %collective-permute-start.17 = (f32[48,128]{1,0:T(8,128)S(1)}, f32[48,128]{1,0:T(8,128)S(1)}, u32[]{:S(2)}, u32[]{:S(2)}) collective-permute-start(f32[48,128]{1,0:T(8,128)S(1)} %get-tuple-element.160.refs_1_), channel_id=1, source_target_pairs={{0,24},{1,25},{2,26},{3,27},{4,28},{5,29},{6,30},{7,31},{8,16},{9,... | collective-permute-start | bytes 73736 | tf_op jit(solution)/shard_map/ppermute | solution.py:466
  75.6 4.7 %collective-permute-start.16 = (f32[48,128]{1,0:T(8,128)S(1)}, f32[48,128]{1,0:T(8,128)S(1)}, u32[]{:S(2)}, u32[]{:S(2)}) collective-permute-start(f32[48,128]{1,0:T(8,128)S(1)} %get-tuple-element.160.refs_1_), channel_id=1, source_target_pairs={{0,16},{1,17},{2,18},{3,19},{4,20},{5,21},{6,22},{7,23},{8,24},{9,... | collective-permute-start | bytes 73736 | tf_op jit(solution)/shard_map/ppermute | solution.py:466
  75.6 4.7 %collective-permute-start.15 = (f32[48,128]{1,0:T(8,128)S(1)}, f32[48,128]{1,0:T(8,128)S(1)}, u32[]{:S(2)}, u32[]{:S(2)}) collective-permute-start(f32[48,128]{1,0:T(8,128)S(1)} %get-tuple-element.160.refs_1_), channel_id=1, source_target_pairs={{0,8},{1,9},{2,10},{3,11},{4,12},{5,13},{6,14},{7,15},{8,0},{9,1},... | collective-permute-start | bytes 73736 | tf_op jit(solution)/shard_map/ppermute | solution.py:466
  85.8 13.9 %collective-permute-start.26 = (f32[32,512]{1,0:T(8,128)S(1)}, f32[32,512]{1,0:T(8,128)S(1)}, u32[]{:S(2)}, u32[]{:S(2)}) collective-permute-start(f32[32,512]{1,0:T(8,128)S(1)} %get-tuple-element.179), channel_id=1, source_target_pairs={{1,2},{3,4},{5,6},{7,8},{9,10},{11,12},{13,14},{15,16},{17,18},{19... | collective-permute-start | bytes 196616 | tf_op jit(solution)/shard_map/ppermute | solution.py:471
  87.0 8.1 %collective-permute-start.22 = (f32[72,128]{1,0:T(8,128)S(1)}, f32[72,128]{1,0:T(8,128)S(1)}, u32[]{:S(2)}, u32[]{:S(2)}) collective-permute-start(f32[72,128]{1,0:T(8,128)S(1)} %get-tuple-element.173.refs_1_), channel_id=1, source_target_pairs={{0,6},{1,7},{2,4},{3,5},{4,2},{5,3},{6,0},{7,1},{8,14},{9,15},{10,... | collective-permute-start | bytes 110600 | tf_op jit(solution)/shard_map/ppermute | solution.py:466
  89.9 5.3 %collective-permute-start.21 = (f32[72,128]{1,0:T(8,128)S(1)}, f32[72,128]{1,0:T(8,128)S(1)}, u32[]{:S(2)}, u32[]{:S(2)}) collective-permute-start(f32[72,128]{1,0:T(8,128)S(1)} %get-tuple-element.173.refs_1_), channel_id=1, source_target_pairs={{0,4},{1,5},{2,6},{3,7},{4,0},{5,1},{6,2},{7,3},{8,12},{9,13},{10,... | collective-permute-start | bytes 110600 | tf_op jit(solution)/shard_map/ppermute | solution.py:466
  95.3 5.6 %collective-permute-start.25 = (f32[40,128]{1,0:T(8,128)S(1)}, f32[40,128]{1,0:T(8,128)S(1)}, u32[]{:S(2)}, u32[]{:S(2)}) collective-permute-start(f32[40,128]{1,0:T(8,128)S(1)} %get-tuple-element.178.refs_1_), channel_id=1, source_target_pairs={{0,24},{1,25},{2,26},{3,27},{4,28},{5,29},{6,30},{7,31},{8,16},{9,... | collective-permute-start | bytes 61448 | tf_op jit(solution)/shard_map/ppermute | solution.py:466
  98.5 4.7 %collective-permute-start.24 = (f32[40,128]{1,0:T(8,128)S(1)}, f32[40,128]{1,0:T(8,128)S(1)}, u32[]{:S(2)}, u32[]{:S(2)}) collective-permute-start(f32[40,128]{1,0:T(8,128)S(1)} %get-tuple-element.178.refs_1_), channel_id=1, source_target_pairs={{0,16},{1,17},{2,18},{3,19},{4,20},{5,21},{6,22},{7,23},{8,24},{9,... | collective-permute-start | bytes 61448 | tf_op jit(solution)/shard_map/ppermute | solution.py:466
  98.5 4.7 %collective-permute-start.23 = (f32[40,128]{1,0:T(8,128)S(1)}, f32[40,128]{1,0:T(8,128)S(1)}, u32[]{:S(2)}, u32[]{:S(2)}) collective-permute-start(f32[40,128]{1,0:T(8,128)S(1)} %get-tuple-element.178.refs_1_), channel_id=1, source_target_pairs={{0,8},{1,9},{2,10},{3,11},{4,12},{5,13},{6,14},{7,15},{8,0},{9,1},... | collective-permute-start | bytes 61448 | tf_op jit(solution)/shard_map/ppermute | solution.py:466
  112.9 5.7 %collective-permute-start.32 = (f32[80,128]{1,0:T(8,128)S(1)}, f32[80,128]{1,0:T(8,128)S(1)}, u32[]{:S(2)}, u32[]{:S(2)}) collective-permute-start(f32[80,128]{1,0:T(8,128)S(1)} %get-tuple-element.211.refs_1_), channel_id=1, source_target_pairs={{0,6},{1,7},{2,4},{3,5},{4,2},{5,3},{6,0},{7,1},{8,14},{9,15},{10,... | collective-permute-start | bytes 122888 | tf_op jit(solution)/shard_map/ppermute | solution.py:466
  122.6 5.6 %collective-permute-start.35 = (f32[48,128]{1,0:T(8,128)S(1)}, f32[48,128]{1,0:T(8,128)S(1)}, u32[]{:S(2)}, u32[]{:S(2)}) collective-permute-start(f32[48,128]{1,0:T(8,128)S(1)} %get-tuple-element.213.refs_1_), channel_id=1, source_target_pairs={{0,24},{1,25},{2,26},{3,27},{4,28},{5,29},{6,30},{7,31},{8,16},{9,... | collective-permute-start | bytes 73736 | tf_op jit(solution)/shard_map/ppermute | solution.py:466
  124.3 4.8 %collective-permute-start.34 = (f32[48,128]{1,0:T(8,128)S(1)}, f32[48,128]{1,0:T(8,128)S(1)}, u32[]{:S(2)}, u32[]{:S(2)}) collective-permute-start(f32[48,128]{1,0:T(8,128)S(1)} %get-tuple-element.213.refs_1_), channel_id=1, source_target_pairs={{0,16},{1,17},{2,18},{3,19},{4,20},{5,21},{6,22},{7,23},{8,24},{9,... | collective-permute-start | bytes 73736 | tf_op jit(solution)/shard_map/ppermute | solution.py:466
  (39 other events, 153.8 us)

commit v2 on v0

--- a/solution.py
+++ b/solution.py
@@ -103,14 +103,13 @@
     for axis in range(3):
         spread = rows[:, axis : axis + 1] - lanes[axis : axis + 1]
         square = spread * spread if square is None else square + spread * spread
-    square = square * (matern_scale * matern_scale)
     scaled = square * lax.rsqrt(jnp.maximum(square, 1e-30))
     return halves((1.0 + scaled) * jnp.exp(-scaled))
 
 
 def fill_matrices(pairs, lane_ref, sub_ref, high_ref, low_ref):
     for matrix, (row_leaf, col_leaf) in enumerate(pairs):
-        lanes = lane_ref[:, col_leaf * LEAF : (col_leaf + 1) * LEAF]
+        lanes = lane_ref[:, col_leaf * LEAF : (col_leaf + 1) * LEAF] * matern_scale
 
         def one(part, carry):
             row_at = pl.multiple_of(row_leaf * LEAF + part * CHUNK, CHUNK)
@@ -127,7 +126,7 @@
     copies = [pltpu.make_async_copy(basis_ref.at[at], raw_ref.at[at], sem_ref.at[at]) for at in range(levels)]
     for copy in copies:
         copy.start()
-    lanes = lane_ref[...]
+    lanes = lane_ref[...] * matern_scale
     sub_ref[...] = jnp.concatenate([lanes, jnp.zeros((8 - lanes.shape[0], lanes.shape[1]), jnp.float32)], axis=0).T
     fill_matrices(pairs, lane_ref, sub_ref, high_ref, low_ref)
     for at, copy in enumerate(copies):
@@ -139,8 +138,8 @@
 def edge_matrices(core_ref, rows, sub_ref, paired_ref, other_ref, high_ref, low_ref):
     core = core_ref[0]
     leaves = sub_ref.shape[0] // LEAF
-    paired = paired_ref[:3]
-    other = other_ref[rows : rows + 3]
+    paired = paired_ref[:3] * matern_scale
+    other = other_ref[rows : rows + 3] * matern_scale
     lanes = [chosen(core, paired, other), chosen(core, other, paired)]
 
     for side in range(2):
@@ -473,17 +472,17 @@
     def down(field, *tile):
         shapes = [f32(rows, LOCAL * LANES), f32(crossing * own, LANES)]
         shapes = shapes + [f32(EDGE_BLOCKS * rows + crossing * own, LANES)] + list(tile)
-        return call(down_kernel, shapes, core, field, high, low, scalars=1, flops=FLOPS)
+        return call(down_kernel, shapes, core, field, high, low, scalars=1, flops=FLOPS if opening else 0)
 
     def inner(half, field):
         args = [weights, field, nugget, *diagonal[half], *beside]
         body = functools.partial(inner_kernel, half)
-        return call(body, [f32(rows, width // 2)], *args, flops=FLOPS // 2)[0]
+        return call(body, [f32(rows, width // 2)], *args, flops=FLOPS // 2 if opening else 0)[0]
 
     def edge(paired, other, front, back, *more):
         shapes = [f32(rows, width)] + ([f32(PRODUCTS_TILE, LANES)] if more else [])
         args = [core, weights, paired, other, *outside, front, back, *more]
-        return call(functools.partial(edge_kernel, bool(more)), shapes, *args, scalars=1, flops=FLOPS // 3)
+        return call(functools.partial(edge_kernel, bool(more)), shapes, *args, scalars=1, flops=FLOPS // 3 if opening else 0)
 
     def chain(products, final, keep, got, tile, beside_steps, r_skel=None, d_skel=None, r_sib=(), d_sib=()):
         depth = PRODUCTS_TILE if products else NORM_TILE
@@ -568,7 +567,7 @@
         args = after(message, turned, paired_coords, other)
         return call(body, [bf16(2, LEAF, LEAF)] * 2, core, *args, scalars=1, flops=FLOPS)
 
-    solution, r, carried = None, rhs, None
+    solution, r, carried, opening = None, rhs, None, True
     for step in range(0, ITERS, 2):
         first, last = step == 0, step + 2 == ITERS
         r_local, keep, part, tile = down(r, f32(NORM_TILE, LANES))
@@ -605,7 +604,7 @@
             w, state, other, d, q, d_skel, d_local, *d_sib = call(
                 body, outs, *args, scalars=1, flops=FLOPS // 2
             )
-        r_skel = message
+        r_skel, opening = message, False
         other = halo(other)
         q_local, keep, part = down(q)
         got = swap(part, 1)

time: 123 us -> 120 us (0.976)
  starting transfers between devices: 50.6 us -> 48 us
    ppermute x33, starting transfers between devices: 47.4 us -> 44.9 us  [swap(): lax.ppermute(value, BOTH, [(source, source ^ mask) for source in range(de...]
  transfers between devices with their start and end apart: 37 -> 37, of which waited for: 19 -> 20; matrix products, arithmetic and copies ran while one was open for 0% -> 0% of each run, Pallas kernels for 21% -> 23%
where the time goes in v2:
time: 120 us
  starting transfers between devices  48 us (40%)
  Pallas kernels  44.2 us (37%)
  waiting for transfers between devices  21.3 us (18%)
  local copies, waits for them, and re-layouts  5.05 us (4%)
    ppermute x33, starting transfers between devices, swap(): lax.ppermute(value, BOTH, [(source, source ^ mask) for source in range(de...  44.9 us
    pallas_call x35, Pallas kernels, call(): pl.pallas_call(body, out_shape=outs, in_specs=[whole(pltpu.SMEM)] * scala...  39.3 us
    ppermute x33, waiting for transfers between devices, swap(): lax.ppermute(value, BOTH, [(source, source ^ mask) for source in range(de...  21.3 us
    pallas_call x1, Pallas kernels, per_device(): pl.pallas_call(functools.partial(setup_kernel, pairs), out_shape=[bf16(ha...  4.93 us
    unnamed x26, local copies, waits for them, and re-layouts  4.8 us
    ppermute x4, starting transfers between devices, halo(): lax.ppermute(other, BOTH, outward + [(target, source) for source, target...  3.16 us
  transfers between devices with their start and end apart: 37, of which 20 were waited for; matrix products, arithmetic and copies ran while one was open for 0% of the time, Pallas kernels for 23%

profile of v2, /device:TPU:0, one launch (start us, length us, event | category | flops | bytes accessed | tf_op | source)
XLA Modules:
  0.0 119.9 jit_solution(12290736773089373200)
XLA Ops:
  4.4 4.9 %shard_map.68 = (bf16[2,512,512]{2,1,0:T(8,128)(2,1)S(1)}, bf16[2,512,512]{2,1,0:T(8,128)(2,1)S(1)}, bf16[896,2048]{1,0:T(8,128)(2,1)S(1)}, bf16[896,2048]{1,0:T(8,128)(2,1)S(1)}, f32[2048,8]{1,0:T(8,128)}) custom-call(f32[3,2048]{1,0:T(4,128)S(1)} %copy-done.8, f32[7,128,2048]{2,1,0:T(8,128)} %basis_ref.1), custom_call_target="tpu_custom_call" | custom-call | flops 3000000000 | bytes 1048576 | tf_op jit(solution)/shard_map/pallas_call | solution.py:536
  9.4 2.3 %shard_map.69 = (f32[32,384]{1,0:T(8,128)S(1)}, f32[80,128]{1,0:T(8,128)S(1)}, f32[208,128]{1,0:T(8,128)S(1)}, f32[8,128]{1,0:T(8,128)S(1)}) custom-call(s32[1]{0:T(128)S(6)} %select_n.15.core_ref.refs_0_, f32[32,2048]{1,0:T(8,128)S(1)} %copy-done.5, bf16[896,2048]{1,0:T(8,128)(2,1)S(1)} %get-tuple-element.111.high_ref.refs_1_, ...), custom_call_target="tpu_custom_call" | custom-call | flops 3000000000 | bytes 1048576 | tf_op jit(solution)/shard_map/pallas_call | solution.py:83
  12.3 3.9 %collective-permute-start = (f32[208,128]{1,0:T(8,128)S(1)}, f32[208,128]{1,0:T(8,128)S(1)}, u32[]{:S(2)}, u32[]{:S(2)}) collective-permute-start(f32[208,128]{1,0:T(8,128)S(1)} %get-tuple-element.113), channel_id=1, source_target_pairs={{0,1},{1,0},{2,3},{3,2},{4,5},{5,4},{6,7},{7,6},{8,9},{9,8},{10,11... | collective-permute-start | bytes 319496 | tf_op jit(solution)/shard_map/ppermute | solution.py:465
  17.2 2.5 %collective-permute-start.4 = (f32[72,128]{1,0:T(8,128)S(1)}, f32[72,128]{1,0:T(8,128)S(1)}, u32[]{:S(2)}, u32[]{:S(2)}) collective-permute-start(f32[72,128]{1,0:T(8,128)S(1)} %get-tuple-element.117.refs_1_), channel_id=1, source_target_pairs={{0,6},{1,7},{2,4},{3,5},{4,2},{5,3},{6,0},{7,1},{8,14},{9,15},{10,... | collective-permute-start | bytes 110600 | tf_op jit(solution)/shard_map/ppermute | solution.py:465
  21.9 6.5 %shard_map.72 = (bf16[2,512,512]{2,1,0:T(8,128)(2,1)S(1)}, bf16[2,512,512]{2,1,0:T(8,128)(2,1)S(1)}, bf16[3,512,512]{2,1,0:T(8,128)(2,1)S(1)}, bf16[3,512,512]{2,1,0:T(8,128)(2,1)S(1)}) custom-call(f32[3,2048]{1,0:T(4,128)S(1)} %copy-done.9, f32[2048,8]{1,0:T(8,128)S(1)} %copy-done.10), custom_call_target="tpu_custom_call" | custom-call | flops 6000000000 | bytes 1048576 | tf_op jit(solution)/shard_map/pallas_call | solution.py:83
  28.5 4.8 %collective-permute-start.7 = (f32[40,128]{1,0:T(8,128)S(1)}, f32[40,128]{1,0:T(8,128)S(1)}, u32[]{:S(2)}, u32[]{:S(2)}) collective-permute-start(f32[40,128]{1,0:T(8,128)S(1)} %get-tuple-element.128.refs_1_), channel_id=1, source_target_pairs={{0,24},{1,25},{2,26},{3,27},{4,28},{5,29},{6,30},{7,31},{8,16},{9,... | collective-permute-start | bytes 61448 | tf_op jit(solution)/shard_map/ppermute | solution.py:465
  33.9 2.6 %shard_map.74 = (bf16[2,512,512]{2,1,0:T(8,128)(2,1)S(1)}, bf16[2,512,512]{2,1,0:T(8,128)(2,1)S(1)}) custom-call(s32[1]{0:T(128)S(6)} %select_n.15.core_ref.refs_0_, f32[2048,8]{1,0:T(8,128)S(1)} %copy-done.11, f32[8,512]{1,0:T(8,128)S(1)} %collective-permute-done.8.refs_1_, f32[40,512]{1,0:T(8,128)S(1)} %collective-permute-done.1.refs_2_.refs_3_), custom_call_target="tpu_custom_call" | custom-call | flops 3000000000 | bytes 1048576 | tf_op jit(solution)/shard_map/pallas_call | solution.py:83
  42.3 2.3 %shard_map.80 = (f32[32,384]{1,0:T(8,128)S(1)}, f32[80,128]{1,0:T(8,128)S(1)}, f32[208,128]{1,0:T(8,128)S(1)}) custom-call(s32[1]{0:T(128)S(6)} %select_n.15.core_ref.refs_0_, f32[32,2048]{1,0:T(8,128)S(1)} %get-tuple-element.151.field_ref.refs_9_.refs_11_.refs_8_.refs_10_, bf16[896,2048]{1,0:T(8,128)(2,1)S(1)} %copy-done.1, bf16[896,2048]{1,0:T(8,128)(2,1)S(1)} %copy-done.3), custom_call_target="tpu_custom_call" | custom-call | bytes 1048576 | tf_op jit(solution)/shard_map/pallas_call | solution.py:83
  49.2 3.9 %collective-permute-start.14 = (f32[80,128]{1,0:T(8,128)S(1)}, f32[80,128]{1,0:T(8,128)S(1)}, u32[]{:S(2)}, u32[]{:S(2)}) collective-permute-start(f32[80,128]{1,0:T(8,128)S(1)} %get-tuple-element.158.refs_1_), channel_id=1, source_target_pairs={{0,6},{1,7},{2,4},{3,5},{4,2},{5,3},{6,0},{7,1},{8,14},{9,15},{10,... | collective-permute-start | bytes 122888 | tf_op jit(solution)/shard_map/ppermute | solution.py:465
  55.0 2.0 %collective-permute-done.13.refs_3_ = f32[80,128]{1,0:T(8,128)S(1)} collective-permute-done((f32[80,128]{1,0:T(8,128)S(1)}, f32[80,128]{1,0:T(8,128)S(1)}, u32[]{:S(2)}, u32[]{:S(2)}) %collective-permute-start.13) | collective-permute-done | bytes 40992 | tf_op jit(solution)/shard_map/ppermute | solution.py:465
  58.6 4.1 %collective-permute-start.17 = (f32[48,128]{1,0:T(8,128)S(1)}, f32[48,128]{1,0:T(8,128)S(1)}, u32[]{:S(2)}, u32[]{:S(2)}) collective-permute-start(f32[48,128]{1,0:T(8,128)S(1)} %get-tuple-element.160.refs_1_), channel_id=1, source_target_pairs={{0,24},{1,25},{2,26},{3,27},{4,28},{5,29},{6,30},{7,31},{8,16},{9,... | collective-permute-start | bytes 73736 | tf_op jit(solution)/shard_map/ppermute | solution.py:465
  64.6 2.9 %collective-permute-done.16.refs_3_ = f32[48,128]{1,0:T(8,128)S(1)} collective-permute-done((f32[48,128]{1,0:T(8,128)S(1)}, f32[48,128]{1,0:T(8,128)S(1)}, u32[]{:S(2)}, u32[]{:S(2)}) %collective-permute-start.16) | collective-permute-done | bytes 24608 | tf_op jit(solution)/shard_map/ppermute | solution.py:465
  69.0 1.5 %shard_map.87 = (f32[32,2048]{1,0:T(8,128)S(1)}, f32[32,2048]{1,0:T(8,128)S(1)}, f32[32,2048]{1,0:T(8,128)S(1)}, f32[32,2048]{1,0:T(8,128)S(1)}, f32[80,128]{1,0...) custom-call(s32[1]{0:T(128)S(6)} %select_n.15.core_ref.refs_0_, ...), custom_call_target="tpu_custom_call" | custom-call | flops 1500000000 | bytes 1048576 | tf_op jit(solution)/shard_map/pallas_call | solution.py:83
  70.5 2.3 %shard_map.88 = (f32[32,384]{1,0:T(8,128)S(1)}, f32[80,128]{1,0:T(8,128)S(1)}, f32[208,128]{1,0:T(8,128)S(1)}, f32[8,128]{1,0:T(8,128)S(1)}) custom-call(s32[1]{0:T(128)S(6)} %select_n.15.core_ref.refs_0_, f32[32,2048]{1,0:T(8,128)S(1)} %get-tuple-element.174.field_ref.refs_7_.refs_8_, bf16[896,2048]{1,0:T(8,128)(2,1)S(1)} %copy-done.1, ...), custom_call_target="tpu_custom_call" | custom-call | bytes 1048576 | tf_op jit(solution)/shard_map/pallas_call | solution.py:83
  74.1 2.9 %collective-permute-start.22 = (f32[72,128]{1,0:T(8,128)S(1)}, f32[72,128]{1,0:T(8,128)S(1)}, u32[]{:S(2)}, u32[]{:S(2)}) collective-permute-start(f32[72,128]{1,0:T(8,128)S(1)} %get-tuple-element.173.refs_1_), channel_id=1, source_target_pairs={{0,6},{1,7},{2,4},{3,5},{4,2},{5,3},{6,0},{7,1},{8,14},{9,15},{10,... | collective-permute-start | bytes 110600 | tf_op jit(solution)/shard_map/ppermute | solution.py:465
  82.5 2.9 %collective-permute-start.25 = (f32[40,128]{1,0:T(8,128)S(1)}, f32[40,128]{1,0:T(8,128)S(1)}, u32[]{:S(2)}, u32[]{:S(2)}) collective-permute-start(f32[40,128]{1,0:T(8,128)S(1)} %get-tuple-element.178.refs_1_), channel_id=1, source_target_pairs={{0,24},{1,25},{2,26},{3,27},{4,28},{5,29},{6,30},{7,31},{8,16},{9,... | collective-permute-start | bytes 61448 | tf_op jit(solution)/shard_map/ppermute | solution.py:465
  85.4 1.6 %collective-permute-start.23 = (f32[40,128]{1,0:T(8,128)S(1)}, f32[40,128]{1,0:T(8,128)S(1)}, u32[]{:S(2)}, u32[]{:S(2)}) collective-permute-start(f32[40,128]{1,0:T(8,128)S(1)} %get-tuple-element.178.refs_1_), channel_id=1, source_target_pairs={{0,8},{1,9},{2,10},{3,11},{4,12},{5,13},{6,14},{7,15},{8,0},{9,1},... | collective-permute-start | bytes 61448 | tf_op jit(solution)/shard_map/ppermute | solution.py:465
  88.1 1.9 %collective-permute-done.24.refs_3_ = f32[40,128]{1,0:T(8,128)S(1)} collective-permute-done((f32[40,128]{1,0:T(8,128)S(1)}, f32[40,128]{1,0:T(8,128)S(1)}, u32[]{:S(2)}, u32[]{:S(2)}) %collective-permute-start.24) | collective-permute-done | bytes 20512 | tf_op jit(solution)/shard_map/ppermute | solution.py:465
  92.8 2.3 %shard_map.96 = (f32[32,384]{1,0:T(8,128)S(1)}, f32[80,128]{1,0:T(8,128)S(1)}, f32[208,128]{1,0:T(8,128)S(1)}) custom-call(s32[1]{0:T(128)S(6)} %select_n.15.core_ref.refs_0_, f32[32,2048]{1,0:T(8,128)S(1)} %get-tuple-element.200.field_ref.refs_9_.refs_10_, bf16[896,2048]{1,0:T(8,128)(2,1)S(1)} %copy-done.1, bf16[896,2048]{1,0:T(8,128)(2,1)S(1)} %copy-done.3), custom_call_target="tpu_custom_call" | custom-call | bytes 1048576 | tf_op jit(solution)/shard_map/pallas_call | solution.py:83
  99.8 4.0 %collective-permute-start.32 = (f32[80,128]{1,0:T(8,128)S(1)}, f32[80,128]{1,0:T(8,128)S(1)}, u32[]{:S(2)}, u32[]{:S(2)}) collective-permute-start(f32[80,128]{1,0:T(8,128)S(1)} %get-tuple-element.211.refs_1_), channel_id=1, source_target_pairs={{0,6},{1,7},{2,4},{3,5},{4,2},{5,3},{6,0},{7,1},{8,14},{9,15},{10,... | collective-permute-start | bytes 122888 | tf_op jit(solution)/shard_map/ppermute | solution.py:465
  105.7 2.0 %collective-permute-done.31.refs_3_ = f32[80,128]{1,0:T(8,128)S(1)} collective-permute-done((f32[80,128]{1,0:T(8,128)S(1)}, f32[80,128]{1,0:T(8,128)S(1)}, u32[]{:S(2)}, u32[]{:S(2)}) %collective-permute-start.31) | collective-permute-done | bytes 40992 | tf_op jit(solution)/shard_map/ppermute | solution.py:465
  109.4 1.9 %collective-permute-start.35 = (f32[48,128]{1,0:T(8,128)S(1)}, f32[48,128]{1,0:T(8,128)S(1)}, u32[]{:S(2)}, u32[]{:S(2)}) collective-permute-start(f32[48,128]{1,0:T(8,128)S(1)} %get-tuple-element.213.refs_1_), channel_id=1, source_target_pairs={{0,24},{1,25},{2,26},{3,27},{4,28},{5,29},{6,30},{7,31},{8,16},{9,... | collective-permute-start | bytes 73736 | tf_op jit(solution)/shard_map/ppermute | solution.py:465
  112.2 1.6 %collective-permute-start.33 = (f32[48,128]{1,0:T(8,128)S(1)}, f32[48,128]{1,0:T(8,128)S(1)}, u32[]{:S(2)}, u32[]{:S(2)}) collective-permute-start(f32[48,128]{1,0:T(8,128)S(1)} %get-tuple-element.213.refs_1_), channel_id=1, source_target_pairs={{0,8},{1,9},{2,10},{3,11},{4,12},{5,13},{6,14},{7,15},{8,0},{9,1},... | collective-permute-start | bytes 73736 | tf_op jit(solution)/shard_map/ppermute | solution.py:465
  117.8 2.2 %shard_map.103 = (f32[32,2048]{1,0:T(8,128)}, f32[32,2048]{1,0:T(8,128)}) custom-call(s32[1]{0:T(128)S(6)} %select_n.15.core_ref.refs_0_, bf16[896,2048]{1,0:T(8,128)(2,1)S(1)} %copy-done.1, bf16[896,2048]{1,0:T(8,128)(2,1)S(1)} %copy-done.3, f32[32,2048]{1,0:T(8,128)S(1)} %get-tuple-element.207.refs_3_, f32[96,128]{1,0:T(8,128)S(1)} %shard_map.102.refs_4_, ...), custom_call_target="tpu_custom_call" | custom-call | flops 1500000000 | bytes 1048576 | tf_op jit(solution)/shard_map/pallas_call | solution.py:83
  (119 shorter events, 49.0 us)
Async XLA Ops:
  2.4 31.6 %collective-permute-start.8 = (f32[8,512]{1,0:T(8,128)S(1)}, f32[8,512]{1,0:T(8,128)S(1)}, u32[]{:S(2)}, u32[]{:S(2)}) collective-permute-start(f32[8,512]{1,0:T(8,128)S(1)} %get-tuple-element.129), channel_id=1, source_target_pairs={{0,1},{1,0},{2,3},{3,2},{4,5},{5,4},{6,7},{7,6},{8,9},{9,8},{10,11... | collective-permute-start | bytes 49160 | tf_op jit(solution)/shard_map/ppermute | solution.py:465
  2.9 31.0 %collective-permute-start.1 = (f32[40,512]{1,0:T(8,128)S(1)}, f32[40,512]{1,0:T(8,128)S(1)}, u32[]{:S(2)}, u32[]{:S(2)}) collective-permute-start(f32[40,512]{1,0:T(8,128)S(1)} %get-tuple-element.114), channel_id=1, source_target_pairs={{1,2},{3,4},{5,6},{7,8},{9,10},{11,12},{13,14},{15,16},{17,18},{19... | collective-permute-start | bytes 245768 | tf_op jit(solution)/shard_map/ppermute | solution.py:470
  12.3 4.8 %collective-permute-start = (f32[208,128]{1,0:T(8,128)S(1)}, f32[208,128]{1,0:T(8,128)S(1)}, u32[]{:S(2)}, u32[]{:S(2)}) collective-permute-start(f32[208,128]{1,0:T(8,128)S(1)} %get-tuple-element.113), channel_id=1, source_target_pairs={{0,1},{1,0},{2,3},{3,2},{4,5},{5,4},{6,7},{7,6},{8,9},{9,8},{10,11... | collective-permute-start | bytes 319496 | tf_op jit(solution)/shard_map/ppermute | solution.py:465
  17.2 11.3 %collective-permute-start.4 = (f32[72,128]{1,0:T(8,128)S(1)}, f32[72,128]{1,0:T(8,128)S(1)}, u32[]{:S(2)}, u32[]{:S(2)}) collective-permute-start(f32[72,128]{1,0:T(8,128)S(1)} %get-tuple-element.117.refs_1_), channel_id=1, source_target_pairs={{0,6},{1,7},{2,4},{3,5},{4,2},{5,3},{6,0},{7,1},{8,14},{9,15},{10,... | collective-permute-start | bytes 110600 | tf_op jit(solution)/shard_map/ppermute | solution.py:465
  19.6 8.8 %collective-permute-start.3 = (f32[72,128]{1,0:T(8,128)S(1)}, f32[72,128]{1,0:T(8,128)S(1)}, u32[]{:S(2)}, u32[]{:S(2)}) collective-permute-start(f32[72,128]{1,0:T(8,128)S(1)} %get-tuple-element.117.refs_1_), channel_id=1, source_target_pairs={{0,4},{1,5},{2,6},{3,7},{4,0},{5,1},{6,2},{7,3},{8,12},{9,13},{10,... | collective-permute-start | bytes 110600 | tf_op jit(solution)/shard_map/ppermute | solution.py:465
  20.1 8.3 %collective-permute-start.2 = (f32[72,128]{1,0:T(8,128)S(1)}, f32[72,128]{1,0:T(8,128)S(1)}, u32[]{:S(2)}, u32[]{:S(2)}) collective-permute-start(f32[72,128]{1,0:T(8,128)S(1)} %get-tuple-element.117.refs_1_), channel_id=1, source_target_pairs={{0,2},{1,3},{2,0},{3,1},{4,6},{5,7},{6,4},{7,5},{8,10},{9,11},{10,... | collective-permute-start | bytes 110600 | tf_op jit(solution)/shard_map/ppermute | solution.py:465
  28.5 10.6 %collective-permute-start.7 = (f32[40,128]{1,0:T(8,128)S(1)}, f32[40,128]{1,0:T(8,128)S(1)}, u32[]{:S(2)}, u32[]{:S(2)}) collective-permute-start(f32[40,128]{1,0:T(8,128)S(1)} %get-tuple-element.128.refs_1_), channel_id=1, source_target_pairs={{0,24},{1,25},{2,26},{3,27},{4,28},{5,29},{6,30},{7,31},{8,16},{9,... | collective-permute-start | bytes 61448 | tf_op jit(solution)/shard_map/ppermute | solution.py:465
  33.3 5.8 %collective-permute-start.6 = (f32[40,128]{1,0:T(8,128)S(1)}, f32[40,128]{1,0:T(8,128)S(1)}, u32[]{:S(2)}, u32[]{:S(2)}) collective-permute-start(f32[40,128]{1,0:T(8,128)S(1)} %get-tuple-element.128.refs_1_), channel_id=1, source_target_pairs={{0,16},{1,17},{2,18},{3,19},{4,20},{5,21},{6,22},{7,23},{8,24},{9,... | collective-permute-start | bytes 61448 | tf_op jit(solution)/shard_map/ppermute | solution.py:465
  33.3 5.8 %collective-permute-start.5 = (f32[40,128]{1,0:T(8,128)S(1)}, f32[40,128]{1,0:T(8,128)S(1)}, u32[]{:S(2)}, u32[]{:S(2)}) collective-permute-start(f32[40,128]{1,0:T(8,128)S(1)} %get-tuple-element.128.refs_1_), channel_id=1, source_target_pairs={{0,8},{1,9},{2,10},{3,11},{4,12},{5,13},{6,14},{7,15},{8,0},{9,1},... | collective-permute-start | bytes 61448 | tf_op jit(solution)/shard_map/ppermute | solution.py:465
  49.2 5.9 %collective-permute-start.14 = (f32[80,128]{1,0:T(8,128)S(1)}, f32[80,128]{1,0:T(8,128)S(1)}, u32[]{:S(2)}, u32[]{:S(2)}) collective-permute-start(f32[80,128]{1,0:T(8,128)S(1)} %get-tuple-element.158.refs_1_), channel_id=1, source_target_pairs={{0,6},{1,7},{2,4},{3,5},{4,2},{5,3},{6,0},{7,1},{8,14},{9,15},{10,... | collective-permute-start | bytes 122888 | tf_op jit(solution)/shard_map/ppermute | solution.py:465
  54.0 4.4 %collective-permute-start.12 = (f32[80,128]{1,0:T(8,128)S(1)}, f32[80,128]{1,0:T(8,128)S(1)}, u32[]{:S(2)}, u32[]{:S(2)}) collective-permute-start(f32[80,128]{1,0:T(8,128)S(1)} %get-tuple-element.158.refs_1_), channel_id=1, source_target_pairs={{0,2},{1,3},{2,0},{3,1},{4,6},{5,7},{6,4},{7,5},{8,10},{9,11},{10,... | collective-permute-start | bytes 122888 | tf_op jit(solution)/shard_map/ppermute | solution.py:465
  58.6 5.9 %collective-permute-start.17 = (f32[48,128]{1,0:T(8,128)S(1)}, f32[48,128]{1,0:T(8,128)S(1)}, u32[]{:S(2)}, u32[]{:S(2)}) collective-permute-start(f32[48,128]{1,0:T(8,128)S(1)} %get-tuple-element.160.refs_1_), channel_id=1, source_target_pairs={{0,24},{1,25},{2,26},{3,27},{4,28},{5,29},{6,30},{7,31},{8,16},{9,... | collective-permute-start | bytes 73736 | tf_op jit(solution)/shard_map/ppermute | solution.py:465
  62.7 4.7 %collective-permute-start.16 = (f32[48,128]{1,0:T(8,128)S(1)}, f32[48,128]{1,0:T(8,128)S(1)}, u32[]{:S(2)}, u32[]{:S(2)}) collective-permute-start(f32[48,128]{1,0:T(8,128)S(1)} %get-tuple-element.160.refs_1_), channel_id=1, source_target_pairs={{0,16},{1,17},{2,18},{3,19},{4,20},{5,21},{6,22},{7,23},{8,24},{9,... | collective-permute-start | bytes 73736 | tf_op jit(solution)/shard_map/ppermute | solution.py:465
  62.7 4.7 %collective-permute-start.15 = (f32[48,128]{1,0:T(8,128)S(1)}, f32[48,128]{1,0:T(8,128)S(1)}, u32[]{:S(2)}, u32[]{:S(2)}) collective-permute-start(f32[48,128]{1,0:T(8,128)S(1)} %get-tuple-element.160.refs_1_), channel_id=1, source_target_pairs={{0,8},{1,9},{2,10},{3,11},{4,12},{5,13},{6,14},{7,15},{8,0},{9,1},... | collective-permute-start | bytes 73736 | tf_op jit(solution)/shard_map/ppermute | solution.py:465
  73.0 13.9 %collective-permute-start.26 = (f32[32,512]{1,0:T(8,128)S(1)}, f32[32,512]{1,0:T(8,128)S(1)}, u32[]{:S(2)}, u32[]{:S(2)}) collective-permute-start(f32[32,512]{1,0:T(8,128)S(1)} %get-tuple-element.179), channel_id=1, source_target_pairs={{1,2},{3,4},{5,6},{7,8},{9,10},{11,12},{13,14},{15,16},{17,18},{19... | collective-permute-start | bytes 196616 | tf_op jit(solution)/shard_map/ppermute | solution.py:470
  74.1 8.2 %collective-permute-start.22 = (f32[72,128]{1,0:T(8,128)S(1)}, f32[72,128]{1,0:T(8,128)S(1)}, u32[]{:S(2)}, u32[]{:S(2)}) collective-permute-start(f32[72,128]{1,0:T(8,128)S(1)} %get-tuple-element.173.refs_1_), channel_id=1, source_target_pairs={{0,6},{1,7},{2,4},{3,5},{4,2},{5,3},{6,0},{7,1},{8,14},{9,15},{10,... | collective-permute-start | bytes 110600 | tf_op jit(solution)/shard_map/ppermute | solution.py:465
  77.0 5.3 %collective-permute-start.21 = (f32[72,128]{1,0:T(8,128)S(1)}, f32[72,128]{1,0:T(8,128)S(1)}, u32[]{:S(2)}, u32[]{:S(2)}) collective-permute-start(f32[72,128]{1,0:T(8,128)S(1)} %get-tuple-element.173.refs_1_), channel_id=1, source_target_pairs={{0,4},{1,5},{2,6},{3,7},{4,0},{5,1},{6,2},{7,3},{8,12},{9,13},{10,... | collective-permute-start | bytes 110600 | tf_op jit(solution)/shard_map/ppermute | solution.py:465
  82.5 5.6 %collective-permute-start.25 = (f32[40,128]{1,0:T(8,128)S(1)}, f32[40,128]{1,0:T(8,128)S(1)}, u32[]{:S(2)}, u32[]{:S(2)}) collective-permute-start(f32[40,128]{1,0:T(8,128)S(1)} %get-tuple-element.178.refs_1_), channel_id=1, source_target_pairs={{0,24},{1,25},{2,26},{3,27},{4,28},{5,29},{6,30},{7,31},{8,16},{9,... | collective-permute-start | bytes 61448 | tf_op jit(solution)/shard_map/ppermute | solution.py:465
  85.3 4.7 %collective-permute-start.24 = (f32[40,128]{1,0:T(8,128)S(1)}, f32[40,128]{1,0:T(8,128)S(1)}, u32[]{:S(2)}, u32[]{:S(2)}) collective-permute-start(f32[40,128]{1,0:T(8,128)S(1)} %get-tuple-element.178.refs_1_), channel_id=1, source_target_pairs={{0,16},{1,17},{2,18},{3,19},{4,20},{5,21},{6,22},{7,23},{8,24},{9,... | collective-permute-start | bytes 61448 | tf_op jit(solution)/shard_map/ppermute | solution.py:465
  85.4 4.7 %collective-permute-start.23 = (f32[40,128]{1,0:T(8,128)S(1)}, f32[40,128]{1,0:T(8,128)S(1)}, u32[]{:S(2)}, u32[]{:S(2)}) collective-permute-start(f32[40,128]{1,0:T(8,128)S(1)} %get-tuple-element.178.refs_1_), channel_id=1, source_target_pairs={{0,8},{1,9},{2,10},{3,11},{4,12},{5,13},{6,14},{7,15},{8,0},{9,1},... | collective-permute-start | bytes 61448 | tf_op jit(solution)/shard_map/ppermute | solution.py:465
  99.8 6.0 %collective-permute-start.32 = (f32[80,128]{1,0:T(8,128)S(1)}, f32[80,128]{1,0:T(8,128)S(1)}, u32[]{:S(2)}, u32[]{:S(2)}) collective-permute-start(f32[80,128]{1,0:T(8,128)S(1)} %get-tuple-element.211.refs_1_), channel_id=1, source_target_pairs={{0,6},{1,7},{2,4},{3,5},{4,2},{5,3},{6,0},{7,1},{8,14},{9,15},{10,... | collective-permute-start | bytes 122888 | tf_op jit(solution)/shard_map/ppermute | solution.py:465
  105.0 4.2 %collective-permute-start.30 = (f32[80,128]{1,0:T(8,128)S(1)}, f32[80,128]{1,0:T(8,128)S(1)}, u32[]{:S(2)}, u32[]{:S(2)}) collective-permute-start(f32[80,128]{1,0:T(8,128)S(1)} %get-tuple-element.211.refs_1_), channel_id=1, source_target_pairs={{0,2},{1,3},{2,0},{3,1},{4,6},{5,7},{6,4},{7,5},{8,10},{9,11},{10,... | collective-permute-start | bytes 122888 | tf_op jit(solution)/shard_map/ppermute | solution.py:465
  109.4 5.7 %collective-permute-start.35 = (f32[48,128]{1,0:T(8,128)S(1)}, f32[48,128]{1,0:T(8,128)S(1)}, u32[]{:S(2)}, u32[]{:S(2)}) collective-permute-start(f32[48,128]{1,0:T(8,128)S(1)} %get-tuple-element.213.refs_1_), channel_id=1, source_target_pairs={{0,24},{1,25},{2,26},{3,27},{4,28},{5,29},{6,30},{7,31},{8,16},{9,... | collective-permute-start | bytes 73736 | tf_op jit(solution)/shard_map/ppermute | solution.py:465
  111.3 4.8 %collective-permute-start.34 = (f32[48,128]{1,0:T(8,128)S(1)}, f32[48,128]{1,0:T(8,128)S(1)}, u32[]{:S(2)}, u32[]{:S(2)}) collective-permute-start(f32[48,128]{1,0:T(8,128)S(1)} %get-tuple-element.213.refs_1_), channel_id=1, source_target_pairs={{0,16},{1,17},{2,18},{3,19},{4,20},{5,21},{6,22},{7,23},{8,24},{9,... | collective-permute-start | bytes 73736 | tf_op jit(solution)/shard_map/ppermute | solution.py:465
  (26 other events, 95.5 us)

commit v3 on v2

--- a/solution.py
+++ b/solution.py
@@ -79,12 +79,13 @@
     return pl.BlockSpec(memory_space=memory)
 
 
-def call(body, outs, *args, scalars=0, flops=0, limit=32):
+def call(body, outs, *args, scalars=0, flops=0, limit=16, scratch=()):
     return pl.pallas_call(
         body,
         out_shape=outs,
         in_specs=[whole(pltpu.SMEM)] * scalars + [whole()] * (len(args) - scalars),
         out_specs=[whole()] * len(outs),
+        scratch_shapes=scratch,
         compiler_params=pltpu.CompilerParams(vmem_limit_bytes=limit * 2**20),
         cost_estimate=pl.CostEstimate(flops=flops, bytes_accessed=2**20, transcendentals=0),
     )(*args)
@@ -107,39 +108,43 @@
     return halves((1.0 + scaled) * jnp.exp(-scaled))
 
 
-def fill_matrices(pairs, lane_ref, sub_ref, high_ref, low_ref):
-    for matrix, (row_leaf, col_leaf) in enumerate(pairs):
-        lanes = lane_ref[:, col_leaf * LEAF : (col_leaf + 1) * LEAF] * matern_scale
+def fill_matrices(groups, lane_ref, sub_ref, high_ref, low_ref):
+    sub_ref[...] = lane_ref[...].T
+    matrix = 0
+    for row_leaf, col_leaves in groups:
+        lanes = [lane_ref[:, leaf * LEAF : (leaf + 1) * LEAF] for leaf in col_leaves]
 
         def one(part, carry):
             row_at = pl.multiple_of(row_leaf * LEAF + part * CHUNK, CHUNK)
             out_at = pl.ds(pl.multiple_of(part * CHUNK, CHUNK), CHUNK)
-            values = matrix_rows(sub_ref[pl.ds(row_at, CHUNK)], lanes)
-            high_ref[matrix, out_at], low_ref[matrix, out_at] = values
+            rows = sub_ref[pl.ds(row_at, CHUNK)]
+            for index, far in enumerate(lanes):
+                values = matrix_rows(rows, far)
+                high_ref[matrix + index, out_at], low_ref[matrix + index, out_at] = values
             return carry
 
         lax.fori_loop(0, LEAF // CHUNK, one, 0, unroll=4)
-
-
-def setup_kernel(pairs, lane_ref, basis_ref, high_ref, low_ref, basis_high_ref, basis_low_ref, sub_ref, raw_ref, sem_ref):
+        matrix += len(col_leaves)
+
+
+def setup_kernel(groups, lane_ref, basis_ref, high_ref, low_ref, basis_high_ref, basis_low_ref, sub_ref, raw_ref, sem_ref):
     levels, rank, _ = basis_ref.shape
     copies = [pltpu.make_async_copy(basis_ref.at[at], raw_ref.at[at], sem_ref.at[at]) for at in range(levels)]
     for copy in copies:
         copy.start()
-    lanes = lane_ref[...] * matern_scale
-    sub_ref[...] = jnp.concatenate([lanes, jnp.zeros((8 - lanes.shape[0], lanes.shape[1]), jnp.float32)], axis=0).T
-    fill_matrices(pairs, lane_ref, sub_ref, high_ref, low_ref)
+    fill_matrices(groups, lane_ref, sub_ref, high_ref, low_ref)
     for at, copy in enumerate(copies):
         copy.wait()
         here = slice(at * rank, (at + 1) * rank)
         basis_high_ref[here], basis_low_ref[here] = halves(raw_ref[at])
 
 
-def edge_matrices(core_ref, rows, sub_ref, paired_ref, other_ref, high_ref, low_ref):
+def edge_matrices(core_ref, rows, lane_ref, paired_ref, other_ref, high_ref, low_ref, sub_ref):
     core = core_ref[0]
-    leaves = sub_ref.shape[0] // LEAF
-    paired = paired_ref[:3] * matern_scale
-    other = other_ref[rows : rows + 3] * matern_scale
+    leaves = lane_ref.shape[1] // LEAF
+    sub_ref[...] = lane_ref[...].T
+    paired = paired_ref[:3]
+    other = other_ref[rows : rows + 3]
     lanes = [chosen(core, paired, other), chosen(core, other, paired)]
 
     for side in range(2):
@@ -161,12 +166,12 @@
     return chosen(core, head, tail), chosen(core, tail, head)
 
 
-def edges_kernel(core_ref, field_ref, coords_ref, paired_ref, other_ref):
+def edges_kernel(core_ref, field_ref, coords_ref, paired_ref, other_ref, lane_ref):
     core = core_ref[0]
-    pad = jnp.zeros((8 - 3, LEAF), jnp.float32)
-    paired, other = sides(core, coords_ref)
-    paired_ref[...] = jnp.concatenate([paired, pad], axis=0)
-    other_ref[...] = jnp.concatenate([sides(core, field_ref)[1], other, pad], axis=0)
+    scaled = coords_ref[...] * matern_scale
+    lane_ref[...] = jnp.concatenate([scaled, jnp.zeros((8 - scaled.shape[0], scaled.shape[1]), jnp.float32)], axis=0)
+    paired_ref[...], other = sides(core, lane_ref)
+    other_ref[...] = jnp.concatenate([sides(core, field_ref)[1], other], axis=0)
 
 
 def down_kernel(core_ref, field_ref, high_ref, low_ref, local_ref, keep_ref, send_ref, *tile_refs):
@@ -211,20 +216,32 @@
     return jnp.broadcast_to(weights.reshape(-1, 1), (weights.size, LEAF))
 
 
-def inner_kernel(half, weights_ref, field_ref, nugget_ref, high_ref, low_ref, pair_high_ref, pair_low_ref, out_ref):
+def row_groups(leaves):
+    return [(leaf, [leaf, leaf + 1] if leaf + 1 < leaves else [leaf]) for leaf in range(leaves)]
+
+
+def inner_kernel(half, weights_ref, field_ref, nugget_ref, *refs):
+    out_ref = refs[-1]
     leaves = weights_ref.shape[0] // WIN
     start = half * (leaves // 2)
     stop = start + leaves // 2
     pieces = {leaf: stacked(leaf_of(field_ref, leaf)) for leaf in range(max(start - 1, 0), min(stop + 1, leaves))}
+    pairs = [(row, col) for row, cols in row_groups(leaves) for col in cols]
+
+    def matrix(row, col):
+        at = pairs.index((row, col))
+        front = refs[0].shape[0]
+        return (refs[0][at], refs[1][at]) if at < front else (refs[2][at - front], refs[3][at - front])
+
     for leaf in range(start, stop):
         at = leaf - start
-        inside = product(pieces[leaf], high_ref[at], low_ref[at], ROWS_COLS)
+        inside = product(pieces[leaf], *matrix(leaf, leaf), ROWS_COLS)
         total = leaf_of(nugget_ref, leaf) * leaf_of(field_ref, leaf) + weight_of(weights_ref, leaf, 0) * inside
         if leaf > 0:
-            before = product(pieces[leaf - 1], pair_high_ref[leaf - 1], pair_low_ref[leaf - 1], ROWS_COLS)
+            before = product(pieces[leaf - 1], *matrix(leaf - 1, leaf), ROWS_COLS)
             total = total + weight_of(weights_ref, leaf, -1) * before
         if leaf < leaves - 1:
-            after = product(pieces[leaf + 1], pair_high_ref[leaf], pair_low_ref[leaf], ROWS_ROWS)
+            after = product(pieces[leaf + 1], *matrix(leaf, leaf + 1), ROWS_ROWS)
             total = total + weight_of(weights_ref, leaf, 1) * after
         out_ref[:, at * LEAF : (at + 1) * LEAF] = total
 
@@ -475,7 +492,7 @@
         return call(down_kernel, shapes, core, field, high, low, scalars=1, flops=FLOPS if opening else 0)
 
     def inner(half, field):
-        args = [weights, field, nugget, *diagonal[half], *beside]
+        args = [weights, field, nugget, *front_matrices, *back_matrices]
         body = functools.partial(inner_kernel, half)
         return call(body, [f32(rows, width // 2)], *args, flops=FLOPS // 2 if opening else 0)[0]
 
@@ -526,46 +543,40 @@
             done = done + levels_out[: len(levels_out) - sibling]
         return message, got[0], results, kept
 
-    paired_coords, other = call(
-        edges_kernel, [f32(8, LEAF), f32(rows + 8, LEAF)], core, rhs, coords, scalars=1
+    paired_coords, other, lanes = call(
+        edges_kernel, [f32(8, LEAF), f32(rows + 8, LEAF), f32(8, width)], core, rhs, coords, scalars=1
     )
     other = halo(other)
     paired_coords = swap(paired_coords, 1)
-    half = leaves // 2
-    pairs = [(leaf, leaf) for leaf in range(half)]
-    *front_diagonal, high, low, turned = pl.pallas_call(
-        functools.partial(setup_kernel, pairs),
-        out_shape=[bf16(half, LEAF, LEAF)] * 2
-        + [pltpu.VMEM((levels * LANES, width), jnp.bfloat16)] * 2
-        + [f32(width, 8)],
+    groups = row_groups(leaves)
+    turned = pltpu.VMEM((width, 8), jnp.float32)
+    *front_matrices, high, low = pl.pallas_call(
+        functools.partial(setup_kernel, groups[:1]),
+        out_shape=[bf16(2, LEAF, LEAF)] * 2 + [pltpu.VMEM((levels * LANES, width), jnp.bfloat16)] * 2,
         in_specs=[whole(), whole(pltpu.HBM)],
-        out_specs=[whole()] * 5,
-        scratch_shapes=[pltpu.VMEM(basis.shape, jnp.float32), pltpu.SemaphoreType.DMA((levels,))],
+        out_specs=[whole()] * 4,
+        scratch_shapes=[turned, pltpu.VMEM(basis.shape, jnp.float32), pltpu.SemaphoreType.DMA((levels,))],
         compiler_params=pltpu.CompilerParams(vmem_limit_bytes=44 * 2**20),
         cost_estimate=pl.CostEstimate(flops=FLOPS, bytes_accessed=2**20, transcendentals=0),
-    )(coords, basis)
-    diagonal = [front_diagonal, None]
-    beside = outside = None
+    )(lanes, basis)
+    back_matrices = outside = None
 
     def after(message, *values):
         return lax.optimization_barrier((message, *values))[1:]
 
     def late_matrices(message):
-        groups = [[(leaf, leaf) for leaf in range(half, leaves)], [(leaf, leaf + 1) for leaf in range(leaves - 1)]]
-
-        def body(lane_ref, sub_ref, *refs):
-            for index, group in enumerate(groups):
-                fill_matrices(group, lane_ref, sub_ref, *refs[2 * index : 2 * index + 2])
-
-        shapes = [bf16(len(group), LEAF, LEAF) for group in groups for _ in range(2)]
-        return call(body, shapes, *after(message, coords, turned), flops=2 * FLOPS)
+        def body(lane_ref, high_ref, low_ref, sub_ref):
+            fill_matrices(groups[1:], lane_ref, sub_ref, high_ref, low_ref)
+
+        shapes = [bf16(2 * leaves - 3, LEAF, LEAF)] * 2
+        return call(body, shapes, *after(message, lanes), flops=2 * FLOPS, scratch=[turned])
 
     def late_edge_matrices(message):
         def body(core_ref, *refs):
             edge_matrices(core_ref, rows, *refs)
 
-        args = after(message, turned, paired_coords, other)
-        return call(body, [bf16(2, LEAF, LEAF)] * 2, core, *args, scalars=1, flops=FLOPS)
+        args = after(message, lanes, paired_coords, other)
+        return call(body, [bf16(2, LEAF, LEAF)] * 2, core, *args, scalars=1, flops=FLOPS, scratch=[turned])
 
     solution, r, carried, opening = None, rhs, None, True
     for step in range(0, ITERS, 2):
@@ -574,8 +585,7 @@
         from_core = got = swap(part, 1)
         if first:
             message, got, results, r_sib = chain(False, False, keep, got, tile, [late_matrices, late_edge_matrices])
-            diagonal[1], beside = results[0][:2], results[0][2:]
-            outside = results[1]
+            back_matrices, outside = results
             (near,) = edge(from_core, other, inner(0, r), inner(1, r))
         else:
             fronts = []

time: 120 us -> 116 us (0.967)
  Pallas kernels: 44.2 us -> 42.2 us
  local copies, waits for them, and re-layouts: 5.05 us -> 3.41 us
    unnamed x26 -> x18, local copies, waits for them, and re-layouts: 4.8 us -> 3.16 us
    pallas_call x1, Pallas kernels: 4.93 us -> 3.49 us  [per_device(): pl.pallas_call(functools.partial(setup_kernel, groups[:1]), out_shape=[bf...]
  transfers between devices with their start and end apart: 37 -> 37, of which waited for: 20 -> 20; matrix products, arithmetic and copies ran while one was open for 0% -> 0% of each run, Pallas kernels for 23% -> 22%
where the time goes in v3:
time: 116 us
  starting transfers between devices  47.9 us (41%)
  Pallas kernels  42.2 us (36%)
  waiting for transfers between devices  21.3 us (18%)
  local copies, waits for them, and re-layouts  3.41 us (3%)
    ppermute x33, starting transfers between devices, swap(): lax.ppermute(value, BOTH, [(source, source ^ mask) for source in range(de...  44.9 us
    pallas_call x35, Pallas kernels, call(): pl.pallas_call(body, out_shape=outs, in_specs=[whole(pltpu.SMEM)] * scala...  38.7 us
    ppermute x33, waiting for transfers between devices, swap(): lax.ppermute(value, BOTH, [(source, source ^ mask) for source in range(de...  21.3 us
    pallas_call x1, Pallas kernels, per_device(): pl.pallas_call(functools.partial(setup_kernel, groups[:1]), out_shape=[bf...  3.49 us
    unnamed x18, local copies, waits for them, and re-layouts  3.16 us
    ppermute x4, starting transfers between devices, halo(): lax.ppermute(other, BOTH, outward + [(target, source) for source, target...  3.02 us
  transfers between devices with their start and end apart: 37, of which 20 were waited for; matrix products, arithmetic and copies ran while one was open for 0% of the time, Pallas kernels for 22%

profile of v3, /device:TPU:0, one launch (start us, length us, event | category | flops | bytes accessed | tf_op | source)
XLA Modules:
  0.0 116.1 jit_solution(8552047135662542628)
XLA Ops:
  3.6 3.5 %shard_map.69 = (bf16[2,512,512]{2,1,0:T(8,128)(2,1)S(1)}, bf16[2,512,512]{2,1,0:T(8,128)(2,1)S(1)}, bf16[896,2048]{1,0:T(8,128)(2,1)S(1)}, bf16[896,2048]{1,0:T(8,128)(2,1)S(1)}) custom-call(f32[8,2048]{1,0:T(8,128)S(1)} %get-tuple-element.122.lane_ref.refs_0_, f32[7,128,2048]{2,1,0:T(8,128)} %basis_ref.1), custom_call_target="tpu_custom_call" | custom-call | flops 3000000000 | bytes 1048576 | tf_op jit(solution)/shard_map/pallas_call | solution.py:553
  7.1 2.3 %shard_map.70 = (f32[32,384]{1,0:T(8,128)S(1)}, f32[80,128]{1,0:T(8,128)S(1)}, f32[208,128]{1,0:T(8,128)S(1)}, f32[8,128]{1,0:T(8,128)S(1)}) custom-call(s32[1]{0:T(128)S(6)} %select_n.15.core_ref.refs_0_, f32[32,2048]{1,0:T(8,128)S(1)} %copy-done.5, bf16[896,2048]{1,0:T(8,128)(2,1)S(1)} %get-tuple-element.107.high_ref.refs_1_, ...), custom_call_target="tpu_custom_call" | custom-call | flops 3000000000 | bytes 1048576 | tf_op jit(solution)/shard_map/pallas_call | solution.py:83
  10.0 3.9 %collective-permute-start = (f32[208,128]{1,0:T(8,128)S(1)}, f32[208,128]{1,0:T(8,128)S(1)}, u32[]{:S(2)}, u32[]{:S(2)}) collective-permute-start(f32[208,128]{1,0:T(8,128)S(1)} %get-tuple-element.109), channel_id=1, source_target_pairs={{0,1},{1,0},{2,3},{3,2},{4,5},{5,4},{6,7},{7,6},{8,9},{9,8},{10,11... | collective-permute-start | bytes 319496 | tf_op jit(solution)/shard_map/ppermute | solution.py:482
  14.8 2.5 %collective-permute-start.4 = (f32[72,128]{1,0:T(8,128)S(1)}, f32[72,128]{1,0:T(8,128)S(1)}, u32[]{:S(2)}, u32[]{:S(2)}) collective-permute-start(f32[72,128]{1,0:T(8,128)S(1)} %get-tuple-element.113.refs_1_), channel_id=1, source_target_pairs={{0,6},{1,7},{2,4},{3,5},{4,2},{5,3},{6,0},{7,1},{8,14},{9,15},{10,... | collective-permute-start | bytes 110600 | tf_op jit(solution)/shard_map/ppermute | solution.py:482
  18.3 5.6 %shard_map.72 = (bf16[5,512,512]{2,1,0:T(8,128)(2,1)S(1)}, bf16[5,512,512]{2,1,0:T(8,128)(2,1)S(1)}) custom-call(f32[8,2048]{1,0:T(8,128)S(1)} %get-tuple-element.122.lane_ref.refs_0_), custom_call_target="tpu_custom_call" | custom-call | flops 6000000000 | bytes 1048576 | tf_op jit(solution)/shard_map/pallas_call | solution.py:83
  24.0 4.8 %collective-permute-start.7 = (f32[40,128]{1,0:T(8,128)S(1)}, f32[40,128]{1,0:T(8,128)S(1)}, u32[]{:S(2)}, u32[]{:S(2)}) collective-permute-start(f32[40,128]{1,0:T(8,128)S(1)} %get-tuple-element.120.refs_1_), channel_id=1, source_target_pairs={{0,24},{1,25},{2,26},{3,27},{4,28},{5,29},{6,30},{7,31},{8,16},{9,... | collective-permute-start | bytes 61448 | tf_op jit(solution)/shard_map/ppermute | solution.py:482
  29.4 3.0 %shard_map.74 = (bf16[2,512,512]{2,1,0:T(8,128)(2,1)S(1)}, bf16[2,512,512]{2,1,0:T(8,128)(2,1)S(1)}) custom-call(s32[1]{0:T(128)S(6)} %select_n.15.core_ref.refs_0_, f32[8,2048]{1,0:T(8,128)S(1)} %get-tuple-element.122.lane_ref.refs_0_, f32[8,512]{1,0:T(8,128)S(1)} %collective-permute-done.8.refs_1_, f32[40,512]{1,0:T(8,128)S(1)} %collective-permute-done.1.refs_2_.refs_3_), custom_call_target="tpu_custom_call" | custom-call | flops 3000000000 | bytes 1048576 | tf_op jit(solution)/shard_map/pallas_call | solution.py:83
  38.5 2.3 %shard_map.80 = (f32[32,384]{1,0:T(8,128)S(1)}, f32[80,128]{1,0:T(8,128)S(1)}, f32[208,128]{1,0:T(8,128)S(1)}) custom-call(s32[1]{0:T(128)S(6)} %select_n.15.core_ref.refs_0_, f32[32,2048]{1,0:T(8,128)S(1)} %get-tuple-element.141.field_ref.refs_9_.refs_11_.refs_8_.refs_10_, bf16[896,2048]{1,0:T(8,128)(2,1)S(1)} %copy-done.1, bf16[896,2048]{1,0:T(8,128)(2,1)S(1)} %copy-done.3), custom_call_target="tpu_custom_call" | custom-call | bytes 1048576 | tf_op jit(solution)/shard_map/pallas_call | solution.py:83
  45.4 3.9 %collective-permute-start.14 = (f32[80,128]{1,0:T(8,128)S(1)}, f32[80,128]{1,0:T(8,128)S(1)}, u32[]{:S(2)}, u32[]{:S(2)}) collective-permute-start(f32[80,128]{1,0:T(8,128)S(1)} %get-tuple-element.148.refs_1_), channel_id=1, source_target_pairs={{0,6},{1,7},{2,4},{3,5},{4,2},{5,3},{6,0},{7,1},{8,14},{9,15},{10,... | collective-permute-start | bytes 122888 | tf_op jit(solution)/shard_map/ppermute | solution.py:482
  51.2 2.0 %collective-permute-done.13.refs_3_ = f32[80,128]{1,0:T(8,128)S(1)} collective-permute-done((f32[80,128]{1,0:T(8,128)S(1)}, f32[80,128]{1,0:T(8,128)S(1)}, u32[]{:S(2)}, u32[]{:S(2)}) %collective-permute-start.13) | collective-permute-done | bytes 40992 | tf_op jit(solution)/shard_map/ppermute | solution.py:482
  54.8 4.1 %collective-permute-start.17 = (f32[48,128]{1,0:T(8,128)S(1)}, f32[48,128]{1,0:T(8,128)S(1)}, u32[]{:S(2)}, u32[]{:S(2)}) collective-permute-start(f32[48,128]{1,0:T(8,128)S(1)} %get-tuple-element.150.refs_1_), channel_id=1, source_target_pairs={{0,24},{1,25},{2,26},{3,27},{4,28},{5,29},{6,30},{7,31},{8,16},{9,... | collective-permute-start | bytes 73736 | tf_op jit(solution)/shard_map/ppermute | solution.py:482
  60.8 2.9 %collective-permute-done.16.refs_3_ = f32[48,128]{1,0:T(8,128)S(1)} collective-permute-done((f32[48,128]{1,0:T(8,128)S(1)}, f32[48,128]{1,0:T(8,128)S(1)}, u32[]{:S(2)}, u32[]{:S(2)}) %collective-permute-start.16) | collective-permute-done | bytes 24608 | tf_op jit(solution)/shard_map/ppermute | solution.py:482
  65.2 1.5 %shard_map.87 = (f32[32,2048]{1,0:T(8,128)S(1)}, f32[32,2048]{1,0:T(8,128)S(1)}, f32[32,2048]{1,0:T(8,128)S(1)}, f32[32,2048]{1,0:T(8,128)S(1)}, f32[80,128]{1,0...) custom-call(s32[1]{0:T(128)S(6)} %select_n.15.core_ref.refs_0_, ...), custom_call_target="tpu_custom_call" | custom-call | flops 1500000000 | bytes 1048576 | tf_op jit(solution)/shard_map/pallas_call | solution.py:83
  66.6 2.3 %shard_map.88 = (f32[32,384]{1,0:T(8,128)S(1)}, f32[80,128]{1,0:T(8,128)S(1)}, f32[208,128]{1,0:T(8,128)S(1)}, f32[8,128]{1,0:T(8,128)S(1)}) custom-call(s32[1]{0:T(128)S(6)} %select_n.15.core_ref.refs_0_, f32[32,2048]{1,0:T(8,128)S(1)} %get-tuple-element.164.field_ref.refs_7_.refs_8_, bf16[896,2048]{1,0:T(8,128)(2,1)S(1)} %copy-done.1, ...), custom_call_target="tpu_custom_call" | custom-call | bytes 1048576 | tf_op jit(solution)/shard_map/pallas_call | solution.py:83
  70.3 2.9 %collective-permute-start.22 = (f32[72,128]{1,0:T(8,128)S(1)}, f32[72,128]{1,0:T(8,128)S(1)}, u32[]{:S(2)}, u32[]{:S(2)}) collective-permute-start(f32[72,128]{1,0:T(8,128)S(1)} %get-tuple-element.163.refs_1_), channel_id=1, source_target_pairs={{0,6},{1,7},{2,4},{3,5},{4,2},{5,3},{6,0},{7,1},{8,14},{9,15},{10,... | collective-permute-start | bytes 110600 | tf_op jit(solution)/shard_map/ppermute | solution.py:482
  78.7 2.9 %collective-permute-start.25 = (f32[40,128]{1,0:T(8,128)S(1)}, f32[40,128]{1,0:T(8,128)S(1)}, u32[]{:S(2)}, u32[]{:S(2)}) collective-permute-start(f32[40,128]{1,0:T(8,128)S(1)} %get-tuple-element.168.refs_1_), channel_id=1, source_target_pairs={{0,24},{1,25},{2,26},{3,27},{4,28},{5,29},{6,30},{7,31},{8,16},{9,... | collective-permute-start | bytes 61448 | tf_op jit(solution)/shard_map/ppermute | solution.py:482
  81.6 1.6 %collective-permute-start.23 = (f32[40,128]{1,0:T(8,128)S(1)}, f32[40,128]{1,0:T(8,128)S(1)}, u32[]{:S(2)}, u32[]{:S(2)}) collective-permute-start(f32[40,128]{1,0:T(8,128)S(1)} %get-tuple-element.168.refs_1_), channel_id=1, source_target_pairs={{0,8},{1,9},{2,10},{3,11},{4,12},{5,13},{6,14},{7,15},{8,0},{9,1},... | collective-permute-start | bytes 61448 | tf_op jit(solution)/shard_map/ppermute | solution.py:482
  84.3 1.9 %collective-permute-done.24.refs_3_ = f32[40,128]{1,0:T(8,128)S(1)} collective-permute-done((f32[40,128]{1,0:T(8,128)S(1)}, f32[40,128]{1,0:T(8,128)S(1)}, u32[]{:S(2)}, u32[]{:S(2)}) %collective-permute-start.24) | collective-permute-done | bytes 20512 | tf_op jit(solution)/shard_map/ppermute | solution.py:482
  89.0 2.3 %shard_map.96 = (f32[32,384]{1,0:T(8,128)S(1)}, f32[80,128]{1,0:T(8,128)S(1)}, f32[208,128]{1,0:T(8,128)S(1)}) custom-call(s32[1]{0:T(128)S(6)} %select_n.15.core_ref.refs_0_, f32[32,2048]{1,0:T(8,128)S(1)} %get-tuple-element.190.field_ref.refs_9_.refs_10_, bf16[896,2048]{1,0:T(8,128)(2,1)S(1)} %copy-done.1, bf16[896,2048]{1,0:T(8,128)(2,1)S(1)} %copy-done.3), custom_call_target="tpu_custom_call" | custom-call | bytes 1048576 | tf_op jit(solution)/shard_map/pallas_call | solution.py:83
  96.0 4.0 %collective-permute-start.32 = (f32[80,128]{1,0:T(8,128)S(1)}, f32[80,128]{1,0:T(8,128)S(1)}, u32[]{:S(2)}, u32[]{:S(2)}) collective-permute-start(f32[80,128]{1,0:T(8,128)S(1)} %get-tuple-element.201.refs_1_), channel_id=1, source_target_pairs={{0,6},{1,7},{2,4},{3,5},{4,2},{5,3},{6,0},{7,1},{8,14},{9,15},{10,... | collective-permute-start | bytes 122888 | tf_op jit(solution)/shard_map/ppermute | solution.py:482
  101.9 2.0 %collective-permute-done.31.refs_3_ = f32[80,128]{1,0:T(8,128)S(1)} collective-permute-done((f32[80,128]{1,0:T(8,128)S(1)}, f32[80,128]{1,0:T(8,128)S(1)}, u32[]{:S(2)}, u32[]{:S(2)}) %collective-permute-start.31) | collective-permute-done | bytes 40992 | tf_op jit(solution)/shard_map/ppermute | solution.py:482
  105.6 1.9 %collective-permute-start.35 = (f32[48,128]{1,0:T(8,128)S(1)}, f32[48,128]{1,0:T(8,128)S(1)}, u32[]{:S(2)}, u32[]{:S(2)}) collective-permute-start(f32[48,128]{1,0:T(8,128)S(1)} %get-tuple-element.203.refs_1_), channel_id=1, source_target_pairs={{0,24},{1,25},{2,26},{3,27},{4,28},{5,29},{6,30},{7,31},{8,16},{9,... | collective-permute-start | bytes 73736 | tf_op jit(solution)/shard_map/ppermute | solution.py:482
  108.4 1.6 %collective-permute-start.33 = (f32[48,128]{1,0:T(8,128)S(1)}, f32[48,128]{1,0:T(8,128)S(1)}, u32[]{:S(2)}, u32[]{:S(2)}) collective-permute-start(f32[48,128]{1,0:T(8,128)S(1)} %get-tuple-element.203.refs_1_), channel_id=1, source_target_pairs={{0,8},{1,9},{2,10},{3,11},{4,12},{5,13},{6,14},{7,15},{8,0},{9,1},... | collective-permute-start | bytes 73736 | tf_op jit(solution)/shard_map/ppermute | solution.py:482
  113.9 2.2 %shard_map.103 = (f32[32,2048]{1,0:T(8,128)}, f32[32,2048]{1,0:T(8,128)}) custom-call(s32[1]{0:T(128)S(6)} %select_n.15.core_ref.refs_0_, bf16[896,2048]{1,0:T(8,128)(2,1)S(1)} %copy-done.1, bf16[896,2048]{1,0:T(8,128)(2,1)S(1)} %copy-done.3, f32[32,2048]{1,0:T(8,128)S(1)} %get-tuple-element.197.refs_3_, f32[96,128]{1,0:T(8,128)S(1)} %shard_map.102.refs_4_, ...), custom_call_target="tpu_custom_call" | custom-call | flops 1500000000 | bytes 1048576 | tf_op jit(solution)/shard_map/pallas_call | solution.py:83
  (111 shorter events, 47.3 us)
Async XLA Ops:
  2.4 27.1 %collective-permute-start.8 = (f32[8,512]{1,0:T(8,128)S(1)}, f32[8,512]{1,0:T(8,128)S(1)}, u32[]{:S(2)}, u32[]{:S(2)}) collective-permute-start(f32[8,512]{1,0:T(8,128)S(1)} %get-tuple-element.121), channel_id=1, source_target_pairs={{0,1},{1,0},{2,3},{3,2},{4,5},{5,4},{6,7},{7,6},{8,9},{9,8},{10,11... | collective-permute-start | bytes 49160 | tf_op jit(solution)/shard_map/ppermute | solution.py:482
  2.9 26.5 %collective-permute-start.1 = (f32[40,512]{1,0:T(8,128)S(1)}, f32[40,512]{1,0:T(8,128)S(1)}, u32[]{:S(2)}, u32[]{:S(2)}) collective-permute-start(f32[40,512]{1,0:T(8,128)S(1)} %get-tuple-element.110), channel_id=1, source_target_pairs={{1,2},{3,4},{5,6},{7,8},{9,10},{11,12},{13,14},{15,16},{17,18},{19... | collective-permute-start | bytes 245768 | tf_op jit(solution)/shard_map/ppermute | solution.py:487
  10.0 4.8 %collective-permute-start = (f32[208,128]{1,0:T(8,128)S(1)}, f32[208,128]{1,0:T(8,128)S(1)}, u32[]{:S(2)}, u32[]{:S(2)}) collective-permute-start(f32[208,128]{1,0:T(8,128)S(1)} %get-tuple-element.109), channel_id=1, source_target_pairs={{0,1},{1,0},{2,3},{3,2},{4,5},{5,4},{6,7},{7,6},{8,9},{9,8},{10,11... | collective-permute-start | bytes 319496 | tf_op jit(solution)/shard_map/ppermute | solution.py:482
  14.8 9.1 %collective-permute-start.4 = (f32[72,128]{1,0:T(8,128)S(1)}, f32[72,128]{1,0:T(8,128)S(1)}, u32[]{:S(2)}, u32[]{:S(2)}) collective-permute-start(f32[72,128]{1,0:T(8,128)S(1)} %get-tuple-element.113.refs_1_), channel_id=1, source_target_pairs={{0,6},{1,7},{2,4},{3,5},{4,2},{5,3},{6,0},{7,1},{8,14},{9,15},{10,... | collective-permute-start | bytes 110600 | tf_op jit(solution)/shard_map/ppermute | solution.py:482
  17.3 6.6 %collective-permute-start.3 = (f32[72,128]{1,0:T(8,128)S(1)}, f32[72,128]{1,0:T(8,128)S(1)}, u32[]{:S(2)}, u32[]{:S(2)}) collective-permute-start(f32[72,128]{1,0:T(8,128)S(1)} %get-tuple-element.113.refs_1_), channel_id=1, source_target_pairs={{0,4},{1,5},{2,6},{3,7},{4,0},{5,1},{6,2},{7,3},{8,12},{9,13},{10,... | collective-permute-start | bytes 110600 | tf_op jit(solution)/shard_map/ppermute | solution.py:482
  17.8 6.1 %collective-permute-start.2 = (f32[72,128]{1,0:T(8,128)S(1)}, f32[72,128]{1,0:T(8,128)S(1)}, u32[]{:S(2)}, u32[]{:S(2)}) collective-permute-start(f32[72,128]{1,0:T(8,128)S(1)} %get-tuple-element.113.refs_1_), channel_id=1, source_target_pairs={{0,2},{1,3},{2,0},{3,1},{4,6},{5,7},{6,4},{7,5},{8,10},{9,11},{10,... | collective-permute-start | bytes 110600 | tf_op jit(solution)/shard_map/ppermute | solution.py:482
  24.0 10.9 %collective-permute-start.7 = (f32[40,128]{1,0:T(8,128)S(1)}, f32[40,128]{1,0:T(8,128)S(1)}, u32[]{:S(2)}, u32[]{:S(2)}) collective-permute-start(f32[40,128]{1,0:T(8,128)S(1)} %get-tuple-element.120.refs_1_), channel_id=1, source_target_pairs={{0,24},{1,25},{2,26},{3,27},{4,28},{5,29},{6,30},{7,31},{8,16},{9,... | collective-permute-start | bytes 61448 | tf_op jit(solution)/shard_map/ppermute | solution.py:482
  28.8 6.1 %collective-permute-start.6 = (f32[40,128]{1,0:T(8,128)S(1)}, f32[40,128]{1,0:T(8,128)S(1)}, u32[]{:S(2)}, u32[]{:S(2)}) collective-permute-start(f32[40,128]{1,0:T(8,128)S(1)} %get-tuple-element.120.refs_1_), channel_id=1, source_target_pairs={{0,16},{1,17},{2,18},{3,19},{4,20},{5,21},{6,22},{7,23},{8,24},{9,... | collective-permute-start | bytes 61448 | tf_op jit(solution)/shard_map/ppermute | solution.py:482
  28.8 6.1 %collective-permute-start.5 = (f32[40,128]{1,0:T(8,128)S(1)}, f32[40,128]{1,0:T(8,128)S(1)}, u32[]{:S(2)}, u32[]{:S(2)}) collective-permute-start(f32[40,128]{1,0:T(8,128)S(1)} %get-tuple-element.120.refs_1_), channel_id=1, source_target_pairs={{0,8},{1,9},{2,10},{3,11},{4,12},{5,13},{6,14},{7,15},{8,0},{9,1},... | collective-permute-start | bytes 61448 | tf_op jit(solution)/shard_map/ppermute | solution.py:482
  45.4 5.9 %collective-permute-start.14 = (f32[80,128]{1,0:T(8,128)S(1)}, f32[80,128]{1,0:T(8,128)S(1)}, u32[]{:S(2)}, u32[]{:S(2)}) collective-permute-start(f32[80,128]{1,0:T(8,128)S(1)} %get-tuple-element.148.refs_1_), channel_id=1, source_target_pairs={{0,6},{1,7},{2,4},{3,5},{4,2},{5,3},{6,0},{7,1},{8,14},{9,15},{10,... | collective-permute-start | bytes 122888 | tf_op jit(solution)/shard_map/ppermute | solution.py:482
  50.2 4.4 %collective-permute-start.12 = (f32[80,128]{1,0:T(8,128)S(1)}, f32[80,128]{1,0:T(8,128)S(1)}, u32[]{:S(2)}, u32[]{:S(2)}) collective-permute-start(f32[80,128]{1,0:T(8,128)S(1)} %get-tuple-element.148.refs_1_), channel_id=1, source_target_pairs={{0,2},{1,3},{2,0},{3,1},{4,6},{5,7},{6,4},{7,5},{8,10},{9,11},{10,... | collective-permute-start | bytes 122888 | tf_op jit(solution)/shard_map/ppermute | solution.py:482
  54.8 5.9 %collective-permute-start.17 = (f32[48,128]{1,0:T(8,128)S(1)}, f32[48,128]{1,0:T(8,128)S(1)}, u32[]{:S(2)}, u32[]{:S(2)}) collective-permute-start(f32[48,128]{1,0:T(8,128)S(1)} %get-tuple-element.150.refs_1_), channel_id=1, source_target_pairs={{0,24},{1,25},{2,26},{3,27},{4,28},{5,29},{6,30},{7,31},{8,16},{9,... | collective-permute-start | bytes 73736 | tf_op jit(solution)/shard_map/ppermute | solution.py:482
  58.9 4.7 %collective-permute-start.16 = (f32[48,128]{1,0:T(8,128)S(1)}, f32[48,128]{1,0:T(8,128)S(1)}, u32[]{:S(2)}, u32[]{:S(2)}) collective-permute-start(f32[48,128]{1,0:T(8,128)S(1)} %get-tuple-element.150.refs_1_), channel_id=1, source_target_pairs={{0,16},{1,17},{2,18},{3,19},{4,20},{5,21},{6,22},{7,23},{8,24},{9,... | collective-permute-start | bytes 73736 | tf_op jit(solution)/shard_map/ppermute | solution.py:482
  58.9 4.7 %collective-permute-start.15 = (f32[48,128]{1,0:T(8,128)S(1)}, f32[48,128]{1,0:T(8,128)S(1)}, u32[]{:S(2)}, u32[]{:S(2)}) collective-permute-start(f32[48,128]{1,0:T(8,128)S(1)} %get-tuple-element.150.refs_1_), channel_id=1, source_target_pairs={{0,8},{1,9},{2,10},{3,11},{4,12},{5,13},{6,14},{7,15},{8,0},{9,1},... | collective-permute-start | bytes 73736 | tf_op jit(solution)/shard_map/ppermute | solution.py:482
  69.2 13.9 %collective-permute-start.26 = (f32[32,512]{1,0:T(8,128)S(1)}, f32[32,512]{1,0:T(8,128)S(1)}, u32[]{:S(2)}, u32[]{:S(2)}) collective-permute-start(f32[32,512]{1,0:T(8,128)S(1)} %get-tuple-element.169), channel_id=1, source_target_pairs={{1,2},{3,4},{5,6},{7,8},{9,10},{11,12},{13,14},{15,16},{17,18},{19... | collective-permute-start | bytes 196616 | tf_op jit(solution)/shard_map/ppermute | solution.py:487
  70.3 8.2 %collective-permute-start.22 = (f32[72,128]{1,0:T(8,128)S(1)}, f32[72,128]{1,0:T(8,128)S(1)}, u32[]{:S(2)}, u32[]{:S(2)}) collective-permute-start(f32[72,128]{1,0:T(8,128)S(1)} %get-tuple-element.163.refs_1_), channel_id=1, source_target_pairs={{0,6},{1,7},{2,4},{3,5},{4,2},{5,3},{6,0},{7,1},{8,14},{9,15},{10,... | collective-permute-start | bytes 110600 | tf_op jit(solution)/shard_map/ppermute | solution.py:482
  73.2 5.3 %collective-permute-start.21 = (f32[72,128]{1,0:T(8,128)S(1)}, f32[72,128]{1,0:T(8,128)S(1)}, u32[]{:S(2)}, u32[]{:S(2)}) collective-permute-start(f32[72,128]{1,0:T(8,128)S(1)} %get-tuple-element.163.refs_1_), channel_id=1, source_target_pairs={{0,4},{1,5},{2,6},{3,7},{4,0},{5,1},{6,2},{7,3},{8,12},{9,13},{10,... | collective-permute-start | bytes 110600 | tf_op jit(solution)/shard_map/ppermute | solution.py:482
  78.7 5.6 %collective-permute-start.25 = (f32[40,128]{1,0:T(8,128)S(1)}, f32[40,128]{1,0:T(8,128)S(1)}, u32[]{:S(2)}, u32[]{:S(2)}) collective-permute-start(f32[40,128]{1,0:T(8,128)S(1)} %get-tuple-element.168.refs_1_), channel_id=1, source_target_pairs={{0,24},{1,25},{2,26},{3,27},{4,28},{5,29},{6,30},{7,31},{8,16},{9,... | collective-permute-start | bytes 61448 | tf_op jit(solution)/shard_map/ppermute | solution.py:482
  81.5 4.7 %collective-permute-start.24 = (f32[40,128]{1,0:T(8,128)S(1)}, f32[40,128]{1,0:T(8,128)S(1)}, u32[]{:S(2)}, u32[]{:S(2)}) collective-permute-start(f32[40,128]{1,0:T(8,128)S(1)} %get-tuple-element.168.refs_1_), channel_id=1, source_target_pairs={{0,16},{1,17},{2,18},{3,19},{4,20},{5,21},{6,22},{7,23},{8,24},{9,... | collective-permute-start | bytes 61448 | tf_op jit(solution)/shard_map/ppermute | solution.py:482
  81.6 4.7 %collective-permute-start.23 = (f32[40,128]{1,0:T(8,128)S(1)}, f32[40,128]{1,0:T(8,128)S(1)}, u32[]{:S(2)}, u32[]{:S(2)}) collective-permute-start(f32[40,128]{1,0:T(8,128)S(1)} %get-tuple-element.168.refs_1_), channel_id=1, source_target_pairs={{0,8},{1,9},{2,10},{3,11},{4,12},{5,13},{6,14},{7,15},{8,0},{9,1},... | collective-permute-start | bytes 61448 | tf_op jit(solution)/shard_map/ppermute | solution.py:482
  96.0 6.0 %collective-permute-start.32 = (f32[80,128]{1,0:T(8,128)S(1)}, f32[80,128]{1,0:T(8,128)S(1)}, u32[]{:S(2)}, u32[]{:S(2)}) collective-permute-start(f32[80,128]{1,0:T(8,128)S(1)} %get-tuple-element.201.refs_1_), channel_id=1, source_target_pairs={{0,6},{1,7},{2,4},{3,5},{4,2},{5,3},{6,0},{7,1},{8,14},{9,15},{10,... | collective-permute-start | bytes 122888 | tf_op jit(solution)/shard_map/ppermute | solution.py:482
  101.2 4.2 %collective-permute-start.30 = (f32[80,128]{1,0:T(8,128)S(1)}, f32[80,128]{1,0:T(8,128)S(1)}, u32[]{:S(2)}, u32[]{:S(2)}) collective-permute-start(f32[80,128]{1,0:T(8,128)S(1)} %get-tuple-element.201.refs_1_), channel_id=1, source_target_pairs={{0,2},{1,3},{2,0},{3,1},{4,6},{5,7},{6,4},{7,5},{8,10},{9,11},{10,... | collective-permute-start | bytes 122888 | tf_op jit(solution)/shard_map/ppermute | solution.py:482
  105.6 5.6 %collective-permute-start.35 = (f32[48,128]{1,0:T(8,128)S(1)}, f32[48,128]{1,0:T(8,128)S(1)}, u32[]{:S(2)}, u32[]{:S(2)}) collective-permute-start(f32[48,128]{1,0:T(8,128)S(1)} %get-tuple-element.203.refs_1_), channel_id=1, source_target_pairs={{0,24},{1,25},{2,26},{3,27},{4,28},{5,29},{6,30},{7,31},{8,16},{9,... | collective-permute-start | bytes 73736 | tf_op jit(solution)/shard_map/ppermute | solution.py:482
  107.5 4.8 %collective-permute-start.34 = (f32[48,128]{1,0:T(8,128)S(1)}, f32[48,128]{1,0:T(8,128)S(1)}, u32[]{:S(2)}, u32[]{:S(2)}) collective-permute-start(f32[48,128]{1,0:T(8,128)S(1)} %get-tuple-element.203.refs_1_), channel_id=1, source_target_pairs={{0,16},{1,17},{2,18},{3,19},{4,20},{5,21},{6,22},{7,23},{8,24},{9,... | collective-permute-start | bytes 73736 | tf_op jit(solution)/shard_map/ppermute | solution.py:482
  (22 other events, 66.6 us)
